TPU v7x, 32 devices: a whole 2x2x4 slice. The times are simulated.
32 devices in a mesh: groups: 2 (over y), ops: 16 (over z, x, core).
Axes of the slice: x: 2, y: 2, z: 4, core: 2. Of those that a mesh axis runs over, the one named last changes fastest.
Arguments:
- psi: bfloat16 [32, 128, 128], P(('groups', 'ops')), parts along dimension 0, may hold values from -6 to 6
- left_ops: bfloat16 [512, 128, 128], P(('groups', 'ops')), parts along dimension 0, may hold values from -0.5 to 0.5
- right_ops: bfloat16 [512, 128, 128], P(('groups', 'ops')), parts along dimension 0, may hold values from -0.125 to 0.125
- couplings: int32 [3, 12288], P(None, ('groups', 'ops')), parts along dimension 1, may hold values from 0 to 15, as said below
- live: int32 [32], P(('groups', 'ops')), parts along dimension 0, may hold values from 48 to 384, as said below
Outputs:
- sigma: float32 [32, 128, 128], P(('groups', 'ops')), parts along dimension 0
There are 2 independent parts, one for each index of `groups`. A program takes and returns all parts, laid end to end along the dimension named above; each array names one. Nothing has to cross between parts.
Inputs may be any that keep to these rules, and one draw needn't show every extreme that they name: `couplings`: row 0 lies in 0 to 15, rows 1 and 2 in 0 to 15. Some list has all 384 slots live, and some list only 48.
All inputs are finite; a program needn't handle non-finite values.
Results may differ from a plain program's by a relative error of at most 0.0029.
Values may be sent and summed in bfloat16 or wider, within the bound.
No kernel may reach another device: no remote copies, remote signals or barrier semaphores. Data moves between devices by JAX's collectives and lax.ppermute only.
A program may use at most 128 MiB of HBM per device.

v0:
```python
import jax
import jax.numpy as jnp
from jax import lax
from jax.sharding import PartitionSpec as P


def apply_range(total, whole, coupling_list, left_table, right_table, stop, offset):
    slots = coupling_list.shape[1]
    width = min(128, slots)
    count = total.shape[0]
    table_rows = left_table.shape[0]
    sector_total = whole.shape[0]
    rounds = (jnp.maximum(stop, 0) + width - 1) // width

    def one_block(index, acc):
        begin = index * width
        clamped = jnp.minimum(begin, slots - width)
        part_list = lax.dynamic_slice_in_dim(coupling_list, clamped, width, 1)
        place = clamped + jnp.arange(width, dtype=jnp.int32)
        weight = ((place >= begin) & (place < stop)).astype(jnp.float32)
        block_hot = (
            part_list[0][:, None] == jnp.arange(table_rows, dtype=jnp.int32)[None, :]
        ).astype(jnp.bfloat16)
        source_hot = (
            part_list[1][:, None] == jnp.arange(sector_total, dtype=jnp.int32)[None, :]
        ).astype(jnp.bfloat16)
        left = jnp.einsum(
            "bo,oij->bij", block_hot, left_table, preferred_element_type=jnp.float32
        ).astype(jnp.bfloat16)
        right = jnp.einsum(
            "bo,oij->bij", block_hot, right_table, preferred_element_type=jnp.float32
        ).astype(jnp.bfloat16)
        state = jnp.einsum(
            "bo,oij->bij", source_hot, whole, preferred_element_type=jnp.float32
        ).astype(jnp.bfloat16)
        half = jnp.einsum("bij,bjk->bik", left, state, preferred_element_type=jnp.float32).astype(
            jnp.bfloat16
        )
        term = jnp.einsum("bij,bkj->bik", half, right, preferred_element_type=jnp.float32)
        target = part_list[2] - offset
        target_hot = (target[:, None] == jnp.arange(count, dtype=jnp.int32)[None, :]).astype(
            jnp.float32
        ) * weight[:, None]
        added = jnp.einsum(
            "bt,bij->tij",
            target_hot,
            term,
            precision=lax.Precision.HIGHEST,
            preferred_element_type=jnp.float32,
        )
        return acc + added

    return lax.fori_loop(0, rounds, one_block, total)


def shards(psi, left_ops, right_ops, couplings, live):
    whole = lax.all_gather(psi, "ops", axis=0, tiled=True)
    sector_dim = psi.shape[1]
    sector_total = whole.shape[0]
    mine = live[0]
    segments = (couplings, left_ops, right_ops, jnp.int32(0), mine)
    total = jnp.zeros((sector_total, sector_dim, sector_dim), jnp.float32)
    coupling_list, left_table, right_table, first, stop = segments
    total = apply_range(total, whole, coupling_list, left_table, right_table, stop, 0)
    return lax.psum_scatter(total, "ops", scatter_dimension=0, tiled=True)


def solution(mesh):
    placed = (
        P(("groups", "ops"), None, None),
        P(("groups", "ops"), None, None),
        P(("groups", "ops"), None, None),
        P(None, ("groups", "ops")),
        P(("groups", "ops")),
    )
    return jax.shard_map(
        shards,
        mesh=mesh,
        in_specs=placed,
        out_specs=P(("groups", "ops"), None, None),
        check_vma=False,
    )
```

profile of v0, /device:TPU:0, one launch (start us, length us, event | category | flops | bytes accessed | tf_op | source)
XLA Modules:
  0.0 219.6 jit_solution(5493781713307149478)
XLA Ops:
  6.5 0.0 reduce-scatter.2.cloned.1.call-start
  7.2 24.8 %all_gather.3 = bf16[16,128,128]{2,1,0:T(8,128)(2,1)S(1)} all-gather(bf16[1,128,128]{2,1,0:T(8,128)(2,1)} %param.7), channel_id=1, replica_groups=mesh['groups'=2,'ops'=16] {'ops'}, dimensions={0}, use_global_device_ids=true | all-gather | bytes 557056 | tf_op jit(solution)/shard_map/all_gather | solution.py:57
  32.0 0.1 broadcast_in_dim.2
  32.1 124.5 %while.10 = (s32[]{:T(128)}, f32[16,128,128]{2,0,1:T(8,128)S(1)}, s32[]{:T(128)}, s32[3,384]{1,0:T(4,128)}, s32[]{:T(128)}, /*index=5*/bf16[16,128,128]{2,1,0:T(...) while((s32[]{:T(128)}, f32[16,128,128]{2,0,1:T(8,128)S(1)}, ...), condition=%wide.region_1.2_spmd, body=%wide.region_0.1_spmd.sunk | while | flops 1680091776 | bytes 49816828 | solution.py:53
  32.1 0.0 copy-start
  32.1 0.7 and_convert_fusion.2
  32.8 0.8 constant_dynamic-slice_fusion.2
  33.6 3.2 %fusion.53 = bf16[128,128,128]{2,0,1:T(8,128)(2,1)} fusion(bf16[16,128,128]{2,1,0:T(8,128)(2,1)S(1)} %get-tuple-element.156, s32[128]{0:T(128)S(1)} %get-tuple-element.122), kind=kOutput, calls=%fused_computation.11.clone.1 | convolution fusion | flops 67110912 | bytes 4719104 | tf_op jit(solution)/shard_map/while/body/bo,oij->bij/dot_general | solution.py:33
  36.8 0.0 copy-done
  36.8 3.2 %fusion.52 = bf16[128,128,128]{2,0,1:T(8,128)(2,1)} fusion(bf16[16,128,128]{2,1,0:T(8,128)(2,1)S(1)} %copy-done, s32[128]{0:T(128)S(1)} %get-tuple-element.121), kind=kOutput, calls=%fused_computation.13.clone.1 | convolution fusion | flops 67110912 | bytes 4719104 | tf_op jit(solution)/shard_map/while/body/bo,oij->bij/dot_general | solution.py:27
  40.1 3.2 %fusion.51 = bf16[128,128,128]{2,0,1:T(8,128)(2,1)} fusion(bf16[16,128,128]{2,1,0:T(8,128)(2,1)S(1)} %copy-done.1, s32[128]{0:T(128)S(1)} %get-tuple-element.121), kind=kOutput, calls=%fused_computation.9.clone.1 | convolution fusion | flops 67110912 | bytes 4719104 | tf_op jit(solution)/shard_map/while/body/bo,oij->bij/dot_general | solution.py:30
  43.3 18.0 %fusion.54 = f32[128,128,128]{2,1,0:T(8,128)} fusion(bf16[128,128,128]{2,0,1:T(8,128)(2,1)} %fusion.51, bf16[128,128,128]{2,0,1:T(8,128)(2,1)} %fusion.52, bf16[128,128,128]{2,0,1:T(8,128)(2,1)} %fusion.53), kind=kOutput, calls=%fused_computation.6.clone.1 | convolution fusion | flops 1075838976 | bytes 20971520 | tf_op jit(solution)/shard_map/while/body/bij,bkj->bik/dot_general | solution.py:39
  61.3 12.3 %fusion.55 = f32[16,128,128]{2,0,1:T(8,128)S(1)} fusion(f32[16,128,128]{2,0,1:T(8,128)S(1)} %get-tuple-element.138, f32[128,128,128]{2,1,0:T(8,128)} %fusion.54, f32[128]{0:T(128)S(1)} %and_convert_fusion.2, s32[128]{0:T(128)S(1)} %get-tuple-element.123), kind=kOutput, calls=%fused_computation.8.clone.1 | convolution fusion | flops 402919424 | bytes 10486784 | tf_op jit(solution)/shard_map/while/body/bt,bij->tij/dot_general | solution.py:44
  73.6 0.0 copy-start
  73.6 0.7 and_convert_fusion.2
  74.3 0.8 constant_dynamic-slice_fusion.2
  75.1 3.2 %fusion.53 = bf16[128,128,128]{2,0,1:T(8,128)(2,1)} fusion(bf16[16,128,128]{2,1,0:T(8,128)(2,1)S(1)} %get-tuple-element.156, s32[128]{0:T(128)S(1)} %get-tuple-element.122), kind=kOutput, calls=%fused_computation.11.clone.1 | convolution fusion | flops 67110912 | bytes 4719104 | tf_op jit(solution)/shard_map/while/body/bo,oij->bij/dot_general | solution.py:33
  78.3 3.2 %fusion.52 = bf16[128,128,128]{2,0,1:T(8,128)(2,1)} fusion(bf16[16,128,128]{2,1,0:T(8,128)(2,1)S(1)} %copy-done, s32[128]{0:T(128)S(1)} %get-tuple-element.121), kind=kOutput, calls=%fused_computation.13.clone.1 | convolution fusion | flops 67110912 | bytes 4719104 | tf_op jit(solution)/shard_map/while/body/bo,oij->bij/dot_general | solution.py:27
  81.6 3.2 %fusion.51 = bf16[128,128,128]{2,0,1:T(8,128)(2,1)} fusion(bf16[16,128,128]{2,1,0:T(8,128)(2,1)S(1)} %copy-done.1, s32[128]{0:T(128)S(1)} %get-tuple-element.121), kind=kOutput, calls=%fused_computation.9.clone.1 | convolution fusion | flops 67110912 | bytes 4719104 | tf_op jit(solution)/shard_map/while/body/bo,oij->bij/dot_general | solution.py:30
  84.8 18.0 %fusion.54 = f32[128,128,128]{2,1,0:T(8,128)} fusion(bf16[128,128,128]{2,0,1:T(8,128)(2,1)} %fusion.51, bf16[128,128,128]{2,0,1:T(8,128)(2,1)} %fusion.52, bf16[128,128,128]{2,0,1:T(8,128)(2,1)} %fusion.53), kind=kOutput, calls=%fused_computation.6.clone.1 | convolution fusion | flops 1075838976 | bytes 20971520 | tf_op jit(solution)/shard_map/while/body/bij,bkj->bik/dot_general | solution.py:39
  102.8 12.3 %fusion.55 = f32[16,128,128]{2,0,1:T(8,128)S(1)} fusion(f32[16,128,128]{2,0,1:T(8,128)S(1)} %get-tuple-element.138, f32[128,128,128]{2,1,0:T(8,128)} %fusion.54, f32[128]{0:T(128)S(1)} %and_convert_fusion.2, s32[128]{0:T(128)S(1)} %get-tuple-element.123), kind=kOutput, calls=%fused_computation.8.clone.1 | convolution fusion | flops 402919424 | bytes 10486784 | tf_op jit(solution)/shard_map/while/body/bt,bij->tij/dot_general | solution.py:44
  115.1 0.0 copy-start
  115.1 0.7 and_convert_fusion.2
  115.8 0.8 constant_dynamic-slice_fusion.2
  116.6 3.2 %fusion.53 = bf16[128,128,128]{2,0,1:T(8,128)(2,1)} fusion(bf16[16,128,128]{2,1,0:T(8,128)(2,1)S(1)} %get-tuple-element.156, s32[128]{0:T(128)S(1)} %get-tuple-element.122), kind=kOutput, calls=%fused_computation.11.clone.1 | convolution fusion | flops 67110912 | bytes 4719104 | tf_op jit(solution)/shard_map/while/body/bo,oij->bij/dot_general | solution.py:33
  119.8 3.2 %fusion.52 = bf16[128,128,128]{2,0,1:T(8,128)(2,1)} fusion(bf16[16,128,128]{2,1,0:T(8,128)(2,1)S(1)} %copy-done, s32[128]{0:T(128)S(1)} %get-tuple-element.121), kind=kOutput, calls=%fused_computation.13.clone.1 | convolution fusion | flops 67110912 | bytes 4719104 | tf_op jit(solution)/shard_map/while/body/bo,oij->bij/dot_general | solution.py:27
  123.1 3.2 %fusion.51 = bf16[128,128,128]{2,0,1:T(8,128)(2,1)} fusion(bf16[16,128,128]{2,1,0:T(8,128)(2,1)S(1)} %copy-done.1, s32[128]{0:T(128)S(1)} %get-tuple-element.121), kind=kOutput, calls=%fused_computation.9.clone.1 | convolution fusion | flops 67110912 | bytes 4719104 | tf_op jit(solution)/shard_map/while/body/bo,oij->bij/dot_general | solution.py:30
  126.3 18.0 %fusion.54 = f32[128,128,128]{2,1,0:T(8,128)} fusion(bf16[128,128,128]{2,0,1:T(8,128)(2,1)} %fusion.51, bf16[128,128,128]{2,0,1:T(8,128)(2,1)} %fusion.52, bf16[128,128,128]{2,0,1:T(8,128)(2,1)} %fusion.53), kind=kOutput, calls=%fused_computation.6.clone.1 | convolution fusion | flops 1075838976 | bytes 20971520 | tf_op jit(solution)/shard_map/while/body/bij,bkj->bik/dot_general | solution.py:39
  144.3 12.3 %fusion.55 = f32[16,128,128]{2,0,1:T(8,128)S(1)} fusion(f32[16,128,128]{2,0,1:T(8,128)S(1)} %get-tuple-element.138, f32[128,128,128]{2,1,0:T(8,128)} %fusion.54, f32[128]{0:T(128)S(1)} %and_convert_fusion.2, s32[128]{0:T(128)S(1)} %get-tuple-element.123), kind=kOutput, calls=%fused_computation.8.clone.1 | convolution fusion | flops 402919424 | bytes 10486784 | tf_op jit(solution)/shard_map/while/body/bt,bij->tij/dot_general | solution.py:44
  156.6 1.3 copy.7
  157.9 0.0 reduce-scatter.2.cloned.1.call-update
  157.9 54.8 %reduce-scatter.2.cloned.1.call-done = f32[1,128,128]{2,1,0:T(8,128)} async-done(((f32[16,128,128]{2,1,0:T(8,128)}), f32[1,128,128]{2,1,0:T(8,128)}) %reduce-scatter.2.cloned.1.call-update) | async-done | bytes 65552 | tf_op jit(solution)/shard_map/reduce_scatter | solution.py:65
  (11 shorter events, 0.0 us)
Async XLA Ops:
  6.5 206.2 %reduce-scatter.2.cloned.1.call-start = ((), (), s32[]{:S(2)}) async-start(), calls=%async_computation.1 | async-start | bytes 1114112 | tf_op jit(solution)/shard_map/reduce_scatter | solution.py:65
  32.1 4.7 %copy-start = (bf16[16,128,128]{2,1,0:T(8,128)(2,1)S(1)}, bf16[16,128,128]{2,1,0:T(8,128)(2,1)}, u32[]{:S(2)}) copy-start(bf16[16,128,128]{2,1,0:T(8,128)(2,1)} %get-tuple-element.155) | copy-start | bytes 1572868 | tf_op jit(solution)/shard_map/while
  33.6 6.5 %copy-start.1 = (bf16[16,128,128]{2,1,0:T(8,128)(2,1)S(1)}, bf16[16,128,128]{2,1,0:T(8,128)(2,1)}, u32[]{:S(2)}) copy-start(bf16[16,128,128]{2,1,0:T(8,128)(2,1)} %get-tuple-element.157) | copy-start | bytes 1572868 | tf_op jit(solution)/shard_map/while
  73.6 4.7 %copy-start = (bf16[16,128,128]{2,1,0:T(8,128)(2,1)S(1)}, bf16[16,128,128]{2,1,0:T(8,128)(2,1)}, u32[]{:S(2)}) copy-start(bf16[16,128,128]{2,1,0:T(8,128)(2,1)} %get-tuple-element.155) | copy-start | bytes 1572868 | tf_op jit(solution)/shard_map/while
  75.1 6.5 %copy-start.1 = (bf16[16,128,128]{2,1,0:T(8,128)(2,1)S(1)}, bf16[16,128,128]{2,1,0:T(8,128)(2,1)}, u32[]{:S(2)}) copy-start(bf16[16,128,128]{2,1,0:T(8,128)(2,1)} %get-tuple-element.157) | copy-start | bytes 1572868 | tf_op jit(solution)/shard_map/while
  115.1 4.7 %copy-start = (bf16[16,128,128]{2,1,0:T(8,128)(2,1)S(1)}, bf16[16,128,128]{2,1,0:T(8,128)(2,1)}, u32[]{:S(2)}) copy-start(bf16[16,128,128]{2,1,0:T(8,128)(2,1)} %get-tuple-element.155) | copy-start | bytes 1572868 | tf_op jit(solution)/shard_map/while
  116.6 6.5 %copy-start.1 = (bf16[16,128,128]{2,1,0:T(8,128)(2,1)S(1)}, bf16[16,128,128]{2,1,0:T(8,128)(2,1)}, u32[]{:S(2)}) copy-start(bf16[16,128,128]{2,1,0:T(8,128)(2,1)} %get-tuple-element.157) | copy-start | bytes 1572868 | tf_op jit(solution)/shard_map/while
Sparse Core Ops, SparseCore 0:
  158.0 54.6 reduce-scatter.1
where the time goes:
time: 220 us
  matrix products  120 us (55%)
  waiting for transfers between devices  54.8 us (25%)
  blocking collectives  24.8 us (11%)
  between operations  14.1 us (6%)
  local copies, waits for them, and re-layouts  3.7 us (2%)
    reduce_scatter x1, waiting for transfers between devices, shards(): return lax.psum_scatter(total, 'ops', scatter_dimension=0, tiled=True)  54.8 us
    dot_general x3, matrix products, one_block(): jnp.einsum('bij,bkj->bik', half, right, preferred_element_type=jnp.float32)  53.9 us
    dot_general x3, matrix products, one_block(): jnp.einsum('bt,bij->tij', target_hot, term, precision=lax.Precision.HIGHE...  36.9 us
    all_gather x1, blocking collectives, shards(): whole = lax.all_gather(psi, 'ops', axis=0, tiled=True)  24.8 us
    dot_general x3, matrix products, one_block(): jnp.einsum('bo,oij->bij', block_hot, right_table, preferred_element_type=...  9.71 us
    dot_general x3, matrix products, one_block(): jnp.einsum('bo,oij->bij', source_hot, whole, preferred_element_type=jnp.f...  9.69 us
    dot_general x3, matrix products, one_block(): jnp.einsum('bo,oij->bij', block_hot, left_table, preferred_element_type=j...  9.68 us
  transfers between devices with their start and end apart: 1, of which 1 were waited for; matrix products, arithmetic and copies ran while one was open for 0% of the time, Pallas kernels for 0%

commit v1 on v0

v1 whole, which is shorter than its diff:
```python
import jax
import jax.numpy as jnp
from jax import lax
from jax.experimental import pallas as pl
from jax.experimental.pallas import tpu as pltpu
from jax.sharding import PartitionSpec as P

VMEM_LIMIT = 60 * 1024 * 1024


def transposed_dot(a, b):
    return lax.dot_general(
        a, b, (((1,), (1,)), ((), ())), preferred_element_type=jnp.float32
    )


def table_kernel(nsec, nops, me_ref, live_ref, coup_ref, *refs):
    psi = refs[:nsec]
    left_ref, right_ref = refs[nsec : nsec + 2]
    odd_ref, even_ref = refs[nsec + 2 : nsec + 4]
    half_ref, sum_ref = refs[nsec + 4 :]
    m = left_ref.shape[1]
    me = me_ref[0]

    step = 4
    for s in range(0, nsec, 2):
        pair = jnp.concatenate([psi[s][0], psi[s + 1][0]], axis=1)
        for g in range(0, nops, step):
            rows = left_ref[g : g + step].reshape(step * m, m)
            both = jnp.dot(rows, pair, preferred_element_type=jnp.float32).astype(jnp.bfloat16)
            half_ref[s, g : g + step] = both[:, :m].reshape(step, m, m)
            half_ref[s + 1, g : g + step] = both[:, m:].reshape(step, m, m)

    @pl.loop(0, nsec)
    def _(t):
        sum_ref[t] = jnp.zeros(sum_ref.shape[1:], jnp.float32)

    @pl.loop(0, live_ref[0])
    def _(c):
        g = coup_ref[0, c]
        s = coup_ref[1, c] ^ me
        t = coup_ref[2, c] ^ me
        sum_ref[t, g] += half_ref[s, g].astype(jnp.float32)

    rights = jnp.concatenate([right_ref[g] for g in range(nops)], axis=1)
    for t in range(nsec):
        sums = jnp.concatenate([sum_ref[t, g].astype(jnp.bfloat16) for g in range(nops)], axis=1)
        out = transposed_dot(sums, rights)
        if t % 2:
            odd_ref[t // 2] = out
        else:
            even_ref[t // 2] = out


def by_table(psi_blocks, left_ops, right_ops, couplings, live, me):
    nsec = len(psi_blocks)
    nops, m, _ = left_ops.shape
    vmem = pl.BlockSpec(memory_space=pltpu.VMEM)
    smem = pl.BlockSpec(memory_space=pltpu.SMEM)
    return pl.pallas_call(
        lambda *refs: table_kernel(nsec, nops, *refs),
        out_shape=[jax.ShapeDtypeStruct((nsec // 2, m, m), jnp.float32)] * 2,
        in_specs=[smem] * 3 + [vmem] * (nsec + 2),
        out_specs=[vmem] * 2,
        scratch_shapes=[
            pltpu.VMEM((nsec, nops, m, m), jnp.bfloat16),
            pltpu.VMEM((nsec, nops, m, m), jnp.float32),
        ],
        compiler_params=pltpu.CompilerParams(vmem_limit_bytes=VMEM_LIMIT),
        name="table",
    )(me, live, couplings, *psi_blocks, left_ops, right_ops)


def slot_kernel(live_ref, coup_ref, psi_ref, left_ref, right_ref, out_ref):
    out_ref[...] = jnp.zeros_like(out_ref)

    @pl.loop(0, live_ref[0])
    def _(c):
        g = coup_ref[0, c]
        half = jnp.dot(left_ref[g], psi_ref[coup_ref[1, c]], preferred_element_type=jnp.float32)
        out_ref[coup_ref[2, c]] += transposed_dot(half.astype(jnp.bfloat16), right_ref[g])


def by_slot(whole, left_ops, right_ops, couplings, live):
    vmem = pl.BlockSpec(memory_space=pltpu.VMEM)
    smem = pl.BlockSpec(memory_space=pltpu.SMEM)
    return pl.pallas_call(
        slot_kernel,
        out_shape=jax.ShapeDtypeStruct(whole.shape, jnp.float32),
        in_specs=[smem] * 2 + [vmem] * 3,
        out_specs=vmem,
        compiler_params=pltpu.CompilerParams(vmem_limit_bytes=VMEM_LIMIT),
        name="slots",
    )(live, couplings, whole, left_ops, right_ops)


def swap(x, ops, d):
    return lax.ppermute(x, "ops", [(i, i ^ d) for i in range(ops)])


def shards_small(ops, psi, left_ops, right_ops, couplings, live):
    me = lax.axis_index("ops").astype(jnp.int32)
    blocks = [None] * ops
    blocks[0] = psi
    for d in range(2, ops, 2):
        blocks[d] = swap(psi, ops, d)
    for d in range(0, ops, 2):
        blocks[d + 1] = swap(blocks[d], ops, 1)
    odd, even = by_table(blocks, left_ops, right_ops, couplings, live, me[None])
    chip = even + swap(odd, ops, 1)
    total = chip[0]
    for d in range(2, ops, 2):
        total = total + swap(chip[d // 2].astype(jnp.bfloat16), ops, d).astype(jnp.float32)
    return total[None]


def shards_large(psi, left_ops, right_ops, couplings, live):
    whole = lax.all_gather(psi, "ops", axis=0, tiled=True)
    total = by_slot(whole, left_ops, right_ops, couplings, live)
    return lax.psum_scatter(total, "ops", scatter_dimension=0, tiled=True)


def solution(mesh):
    ops = mesh.shape["ops"]
    placed = (
        P(("groups", "ops"), None, None),
        P(("groups", "ops"), None, None),
        P(("groups", "ops"), None, None),
        P(None, ("groups", "ops")),
        P(("groups", "ops")),
    )

    def shards(psi, *rest):
        small = psi.shape[0] == 1 and ops <= 16 and ops & (ops - 1) == 0
        if small:
            return shards_small(ops, psi, *rest)
        return shards_large(psi, *rest)

    return jax.shard_map(
        shards,
        mesh=mesh,
        in_specs=placed,
        out_specs=P(("groups", "ops"), None, None),
        check_vma=False,
    )
```

time: 220 us -> 52.3 us (0.24)
  matrix products: 120 us -> 0 us
  waiting for transfers between devices: 54.8 us -> 10.1 us
  starting transfers between devices: 0.01 us -> 26.3 us
  blocking collectives: 24.8 us -> 0 us
  between operations: 14.1 us -> 0.85 us
  Pallas kernels: 0 us -> 12.3 us
  local copies, waits for them, and re-layouts: 3.7 us -> 0.6 us
    dot_general x15 -> x0, matrix products: 120 us -> none  [the longest x3 53.9 us: one_block(): jnp.einsum('bij,bkj->bik', half, right, preferred_element_type=jnp.float32)]
    reduce_scatter x1 -> x0, waiting for transfers between devices: 54.8 us -> none  [shards(): return lax.psum_scatter(total, 'ops', scatter_dimension=0, tiled=True)]
    ppermute x0 -> x23, starting transfers between devices: none -> 26.3 us  [swap(): return lax.ppermute(x, 'ops', [(i, i ^ d) for i in range(ops)])]
    all_gather x1 -> x0, blocking collectives: 24.8 us -> none  [shards(): whole = lax.all_gather(psi, 'ops', axis=0, tiled=True)]
    pallas_call x0 -> x1, Pallas kernels: none -> 12.3 us  [by_table(): pl.pallas_call(lambda *refs: table_kernel(nsec, nops, *refs), out_shape=[...]
    ppermute x0 -> x23, waiting for transfers between devices: none -> 10.1 us  [swap(): return lax.ppermute(x, 'ops', [(i, i ^ d) for i in range(ops)])]
    dynamic_slice x3 -> x0, local copies, waits for them, and re-layouts: 2.3 us -> none  [one_block(): part_list = lax.dynamic_slice_in_dim(coupling_list, clamped, width, 1)]
  transfers between devices with their start and end apart: 1 -> 23, of which waited for: 1 -> 8; matrix products, arithmetic and copies ran while one was open for 0% -> 0% of each run, Pallas kernels for 0% -> 0%
where the time goes in v1:
time: 52.3 us; the launch traced here: 51.9 us
  starting transfers between devices  26.3 us (50%)
  Pallas kernels  12.3 us (24%)
  waiting for transfers between devices  10.1 us (19%)
  other arithmetic  1.78 us (3%)
  between operations  0.85 us (2%)
  local copies, waits for them, and re-layouts  0.6 us (1%)
    ppermute x23, starting transfers between devices, swap(): return lax.ppermute(x, 'ops', [(i, i ^ d) for i in range(ops)])  26.3 us
    pallas_call x1, Pallas kernels, by_table(): pl.pallas_call(lambda *refs: table_kernel(nsec, nops, *refs), out_shape=[...  12.3 us
    ppermute x23, waiting for transfers between devices, swap(): return lax.ppermute(x, 'ops', [(i, i ^ d) for i in range(ops)])  10.1 us
    another operation x1, other arithmetic  1.12 us
  transfers between devices with their start and end apart: 23, of which 8 were waited for; matrix products, arithmetic and copies ran while one was open for 0% of the time, Pallas kernels for 0%

profile of v1, /device:TPU:0, one launch (start us, length us, event | category | flops | bytes accessed | tf_op | source)
XLA Modules:
  0.0 51.9 jit_solution(1431897205148256277)
XLA Ops:
  0.0 5.0 %collective-permute-start.11 = (bf16[1,128,128]{2,1,0:T(8,128)(2,1)}, bf16[1,128,128]{2,1,0:T(8,128)(2,1)S(1)}, u32[]{:S(2)}, u32[]{:S(2)}) collective-permute-start(bf16[1,128,128]{2,1,0:T(8,128)(2,1)} %refs_3_.1), channel_id=1, source_target_pairs={{0,12},{1,13},{2,14},{3,15},{4,8},{5,9},{6,10},{7,11},{8,4},{9,5},... | collective-permute-start | bytes 98312 | tf_op jit(solution)/shard_map/ppermute | solution.py:98
  5.0 0.4 collective-permute-start.9
  5.4 3.5 %collective-permute-start.7 = (bf16[1,128,128]{2,1,0:T(8,128)(2,1)}, bf16[1,128,128]{2,1,0:T(8,128)(2,1)S(1)}, u32[]{:S(2)}, u32[]{:S(2)}) collective-permute-start(bf16[1,128,128]{2,1,0:T(8,128)(2,1)} %refs_3_.1), channel_id=1, source_target_pairs={{0,8},{1,9},{2,10},{3,11},{4,12},{5,13},{6,14},{7,15},{8,0},{9,1},... | collective-permute-start | bytes 98312 | tf_op jit(solution)/shard_map/ppermute | solution.py:98
  8.9 2.0 %collective-permute-start.3 = (bf16[1,128,128]{2,1,0:T(8,128)(2,1)}, bf16[1,128,128]{2,1,0:T(8,128)(2,1)S(1)}, u32[]{:S(2)}, u32[]{:S(2)}) collective-permute-start(bf16[1,128,128]{2,1,0:T(8,128)(2,1)} %refs_3_.1), channel_id=1, source_target_pairs={{0,4},{1,5},{2,6},{3,7},{4,0},{5,1},{6,2},{7,3},{8,12},{9,13},{10,... | collective-permute-start | bytes 98312 | tf_op jit(solution)/shard_map/ppermute | solution.py:98
  10.9 1.5 %collective-permute-start.1 = (bf16[1,128,128]{2,1,0:T(8,128)(2,1)}, bf16[1,128,128]{2,1,0:T(8,128)(2,1)S(1)}, u32[]{:S(2)}, u32[]{:S(2)}) collective-permute-start(bf16[1,128,128]{2,1,0:T(8,128)(2,1)} %refs_3_.1), channel_id=1, source_target_pairs={{0,2},{1,3},{2,0},{3,1},{4,6},{5,7},{6,4},{7,5},{8,10},{9,11},{10,... | collective-permute-start | bytes 98312 | tf_op jit(solution)/shard_map/ppermute | solution.py:98
  12.4 0.8 %collective-permute-start.13 = (bf16[1,128,128]{2,1,0:T(8,128)(2,1)}, bf16[1,128,128]{2,1,0:T(8,128)(2,1)S(1)}, u32[]{:S(2)}, u32[]{:S(2)}) collective-permute-start(bf16[1,128,128]{2,1,0:T(8,128)(2,1)} %refs_3_.1), channel_id=1, source_target_pairs={{0,14},{1,15},{2,12},{3,13},{4,10},{5,11},{6,8},{7,9},{8,6},{9,7},... | collective-permute-start | bytes 98312 | tf_op jit(solution)/shard_map/ppermute | solution.py:98
  13.2 0.7 %collective-permute-done.5.refs_9_ = bf16[1,128,128]{2,1,0:T(8,128)(2,1)S(1)} collective-permute-done((bf16[1,128,128]{2,1,0:T(8,128)(2,1)}, bf16[1,128,128]{2,1,0:T(8,128)(2,1)S(1)}, u32[]{:S(2)}, u32[]{:S(2)}) %collective-permute-start.5) | collective-permute-done | bytes 32800 | tf_op jit(solution)/shard_map/ppermute | solution.py:98
  13.9 0.5 collective-permute-start.10
  14.4 0.6 %collective-permute-done.1.refs_5_ = bf16[1,128,128]{2,1,0:T(8,128)(2,1)S(1)} collective-permute-done((bf16[1,128,128]{2,1,0:T(8,128)(2,1)}, bf16[1,128,128]{2,1,0:T(8,128)(2,1)S(1)}, u32[]{:S(2)}, u32[]{:S(2)}) %collective-permute-start.1) | collective-permute-done | bytes 32800 | tf_op jit(solution)/shard_map/ppermute | solution.py:98
  15.1 0.5 collective-permute-start.6
  15.6 3.8 %collective-permute-done.13.refs_17_ = bf16[1,128,128]{2,1,0:T(8,128)(2,1)S(1)} collective-permute-done((bf16[1,128,128]{2,1,0:T(8,128)(2,1)}, bf16[1,128,128]{2,1,0:T(8,128)(2,1)S(1)}, u32[]{:S(2)}, u32[]{:S(2)}) %collective-permute-start.13) | collective-permute-done | bytes 32800 | tf_op jit(solution)/shard_map/ppermute | solution.py:98
  19.3 0.5 collective-permute-start.2
  19.8 0.1 collective-permute-start.14
  20.6 0.1 collective-permute-done.2.refs_6_
  20.7 0.4 collective-permute-done.14.refs_18_
  21.1 0.1 copy-done.10
  21.2 0.0 copy-done.12
  21.2 0.1 copy-done.13
  21.3 0.4 copy-done.14
  21.7 12.3 %table.1 = (f32[8,128,128]{2,1,0:T(8,128)}, f32[8,128,128]{2,1,0:T(8,128)}) custom-call(s32[1]{0:T(128)} %bitcast.refs_0_, s32[1]{0:T(128)S(6)} %copy.6.refs_1_, s32[3,384]{1,0:T(4,128)} %refs_2_.1, bf16[1,128,128]{2,1,0:T(8,128)(2,1)} %refs_3_.1, bf16[1,128,128]{2,1,0:T(8,128)(2,1)} %copy-done.6, bf16[1,128,128]{2,1,0:T(8,128)(2,1)} %copy-done.5, ...), custom_call_target="tpu_custom_call" | custom-call | tf_op jit(solution)/shard_map/table/pallas_call | solution.py:60
  34.0 0.3 collective-permute-start.15
  34.3 1.8 %collective-permute-done.15 = f32[8,128,128]{2,1,0:T(8,128)S(1)} collective-permute-done((f32[8,128,128]{2,1,0:T(8,128)}, f32[8,128,128]{2,1,0:T(8,128)S(1)}, u32[]{:S(2)}, u32[]{:S(2)}) %collective-permute-start.15) | collective-permute-done | bytes 524320 | tf_op jit(solution)/shard_map/ppermute | solution.py:98
  36.1 1.1 %fusion.8 = (bf16[8,128,128]{2,1,0:T(8,128)(2,1)S(1)}, f32[8,128,128]{2,1,0:T(8,128)S(1)}) fusion(f32[8,128,128]{2,1,0:T(8,128)} %get-tuple-element.7, f32[8,128,128]{2,1,0:T(8,128)S(1)} %collective-permute-done.15), kind=kLoop, calls=%fused_computation.16 | loop fusion | flops 262144 | bytes 1835008 | tf_op jit(solution)/shard_map/convert.6
  37.3 1.5 %collective-permute-start.16 = (bf16[128,128]{1,0:T(8,128)(2,1)S(1)}, bf16[128,128]{1,0:T(8,128)(2,1)S(1)}, u32[]{:S(2)}, u32[]{:S(2)}) collective-permute-start(bf16[128,128]{1,0:T(8,128)(2,1)S(1)} %get-tuple-element.11), channel_id=1, source_target_pairs={{0,2},{1,3},{2,0},{3,1},{4,6},{5,7},{6,4},{7,5},{8,10},{9,11},{10,... | collective-permute-start | bytes 98312 | tf_op jit(solution)/shard_map/ppermute | solution.py:98
  38.8 2.9 %collective-permute-start.22 = (bf16[128,128]{1,0:T(8,128)(2,1)S(1)}, bf16[128,128]{1,0:T(8,128)(2,1)S(1)}, u32[]{:S(2)}, u32[]{:S(2)}) collective-permute-start(bf16[128,128]{1,0:T(8,128)(2,1)S(1)} %get-tuple-element.12), channel_id=1, source_target_pairs={{0,14},{1,15},{2,12},{3,13},{4,10},{5,11},{6,8},{7,9},{8,6},{9,7},... | collective-permute-start | bytes 98312 | tf_op jit(solution)/shard_map/ppermute | solution.py:98
  41.6 1.0 %collective-permute-start.21 = (bf16[128,128]{1,0:T(8,128)(2,1)S(1)}, bf16[128,128]{1,0:T(8,128)(2,1)S(1)}, u32[]{:S(2)}, u32[]{:S(2)}) collective-permute-start(bf16[128,128]{1,0:T(8,128)(2,1)S(1)} %get-tuple-element.13), channel_id=1, source_target_pairs={{0,12},{1,13},{2,14},{3,15},{4,8},{5,9},{6,10},{7,11},{8,4},{9,5},... | collective-permute-start | bytes 98312 | tf_op jit(solution)/shard_map/ppermute | solution.py:98
  42.6 3.8 %collective-permute-start.19 = (bf16[128,128]{1,0:T(8,128)(2,1)S(1)}, bf16[128,128]{1,0:T(8,128)(2,1)S(1)}, u32[]{:S(2)}, u32[]{:S(2)}) collective-permute-start(bf16[128,128]{1,0:T(8,128)(2,1)S(1)} %get-tuple-element.15), channel_id=1, source_target_pairs={{0,8},{1,9},{2,10},{3,11},{4,12},{5,13},{6,14},{7,15},{8,0},{9,1},... | collective-permute-start | bytes 98312 | tf_op jit(solution)/shard_map/ppermute | solution.py:98
  46.4 0.5 collective-permute-start.18
  46.9 1.5 %collective-permute-start.17 = (bf16[128,128]{1,0:T(8,128)(2,1)S(1)}, bf16[128,128]{1,0:T(8,128)(2,1)S(1)}, u32[]{:S(2)}, u32[]{:S(2)}) collective-permute-start(bf16[128,128]{1,0:T(8,128)(2,1)S(1)} %get-tuple-element.17), channel_id=1, source_target_pairs={{0,4},{1,5},{2,6},{3,7},{4,0},{5,1},{6,2},{7,3},{8,12},{9,13},{10,... | collective-permute-start | bytes 98312 | tf_op jit(solution)/shard_map/ppermute | solution.py:98
  48.5 0.6 %collective-permute-done.19 = bf16[128,128]{1,0:T(8,128)(2,1)S(1)} collective-permute-done((bf16[128,128]{1,0:T(8,128)(2,1)S(1)}, bf16[128,128]{1,0:T(8,128)(2,1)S(1)}, u32[]{:S(2)}, u32[]{:S(2)}) %collective-permute-start.19) | collective-permute-done | bytes 32800 | tf_op jit(solution)/shard_map/ppermute | solution.py:98
  49.1 2.2 %collective-permute-done.18 = bf16[128,128]{1,0:T(8,128)(2,1)S(1)} collective-permute-done((bf16[128,128]{1,0:T(8,128)(2,1)S(1)}, bf16[128,128]{1,0:T(8,128)(2,1)S(1)}, u32[]{:S(2)}, u32[]{:S(2)}) %collective-permute-start.18) | collective-permute-done | bytes 32800 | tf_op jit(solution)/shard_map/ppermute | solution.py:98
  51.2 0.7 %fusion.7 = f32[1,128,128]{2,1,0:T(8,128)} fusion(f32[8,128,128]{2,1,0:T(8,128)S(1)} %get-tuple-element.10, bf16[128,128]{1,0:T(8,128)(2,1)S(1)} %collective-permute-done.22, bf16[128,128]{1,0:T(8,128)(2,1)S(1)} %collective-permute-done.21, bf16[128,128]{1,0:T(8,128)(2,1)S(1)} %collective-permute-done.20, bf16[128,128]{1,0:T(8,128)(2,1)S(1)} %collective-permute-done.19, ...), kind=kLoop, calls=%fused_computation.8 | loop fusion | flops 229376 | bytes 360448 | tf_op jit(solution)/shard_map/broadcast_in_dim | solution.py:114
  (48 shorter events, 0.1 us)
Async XLA Ops:
  0.0 10.9 %collective-permute-start.11 = (bf16[1,128,128]{2,1,0:T(8,128)(2,1)}, bf16[1,128,128]{2,1,0:T(8,128)(2,1)S(1)}, u32[]{:S(2)}, u32[]{:S(2)}) collective-permute-start(bf16[1,128,128]{2,1,0:T(8,128)(2,1)} %refs_3_.1), channel_id=1, source_target_pairs={{0,12},{1,13},{2,14},{3,15},{4,8},{5,9},{6,10},{7,11},{8,4},{9,5},... | collective-permute-start | bytes 98312 | tf_op jit(solution)/shard_map/ppermute | solution.py:98
  5.0 7.4 %collective-permute-start.9 = (bf16[1,128,128]{2,1,0:T(8,128)(2,1)}, bf16[1,128,128]{2,1,0:T(8,128)(2,1)S(1)}, u32[]{:S(2)}, u32[]{:S(2)}) collective-permute-start(bf16[1,128,128]{2,1,0:T(8,128)(2,1)} %refs_3_.1), channel_id=1, source_target_pairs={{0,10},{1,11},{2,8},{3,9},{4,14},{5,15},{6,12},{7,13},{8,2},{9,3},... | collective-permute-start | bytes 98312 | tf_op jit(solution)/shard_map/ppermute | solution.py:98
  5.4 7.0 %collective-permute-start.7 = (bf16[1,128,128]{2,1,0:T(8,128)(2,1)}, bf16[1,128,128]{2,1,0:T(8,128)(2,1)S(1)}, u32[]{:S(2)}, u32[]{:S(2)}) collective-permute-start(bf16[1,128,128]{2,1,0:T(8,128)(2,1)} %refs_3_.1), channel_id=1, source_target_pairs={{0,8},{1,9},{2,10},{3,11},{4,12},{5,13},{6,14},{7,15},{8,0},{9,1},... | collective-permute-start | bytes 98312 | tf_op jit(solution)/shard_map/ppermute | solution.py:98
  8.9 5.0 %collective-permute-start.5 = (bf16[1,128,128]{2,1,0:T(8,128)(2,1)}, bf16[1,128,128]{2,1,0:T(8,128)(2,1)S(1)}, u32[]{:S(2)}, u32[]{:S(2)}) collective-permute-start(bf16[1,128,128]{2,1,0:T(8,128)(2,1)} %refs_3_.1), channel_id=1, source_target_pairs={{0,6},{1,7},{2,4},{3,5},{4,2},{5,3},{6,0},{7,1},{8,14},{9,15},{10,... | collective-permute-start | bytes 98312 | tf_op jit(solution)/shard_map/ppermute | solution.py:98
  8.9 5.0 %collective-permute-start.3 = (bf16[1,128,128]{2,1,0:T(8,128)(2,1)}, bf16[1,128,128]{2,1,0:T(8,128)(2,1)S(1)}, u32[]{:S(2)}, u32[]{:S(2)}) collective-permute-start(bf16[1,128,128]{2,1,0:T(8,128)(2,1)} %refs_3_.1), channel_id=1, source_target_pairs={{0,4},{1,5},{2,6},{3,7},{4,0},{5,1},{6,2},{7,3},{8,12},{9,13},{10,... | collective-permute-start | bytes 98312 | tf_op jit(solution)/shard_map/ppermute | solution.py:98
  10.9 10.2 %copy-start = (bf16[1,128,128]{2,1,0:T(8,128)(2,1)}, bf16[1,128,128]{2,1,0:T(8,128)(2,1)S(1)}, u32[]{:S(2)}) copy-start(bf16[1,128,128]{2,1,0:T(8,128)(2,1)S(1)} %collective-permute-done.11.refs_15_) | copy-start | bytes 98308
  10.9 4.1 %collective-permute-start.1 = (bf16[1,128,128]{2,1,0:T(8,128)(2,1)}, bf16[1,128,128]{2,1,0:T(8,128)(2,1)S(1)}, u32[]{:S(2)}, u32[]{:S(2)}) collective-permute-start(bf16[1,128,128]{2,1,0:T(8,128)(2,1)} %refs_3_.1), channel_id=1, source_target_pairs={{0,2},{1,3},{2,0},{3,1},{4,6},{5,7},{6,4},{7,5},{8,10},{9,11},{10,... | collective-permute-start | bytes 98312 | tf_op jit(solution)/shard_map/ppermute | solution.py:98
  12.4 8.7 %copy-start.1 = (bf16[1,128,128]{2,1,0:T(8,128)(2,1)}, bf16[1,128,128]{2,1,0:T(8,128)(2,1)S(1)}, u32[]{:S(2)}) copy-start(bf16[1,128,128]{2,1,0:T(8,128)(2,1)S(1)} %collective-permute-done.9.refs_13_) | copy-start | bytes 98308
  12.4 2.6 %collective-permute-start = (bf16[1,128,128]{2,1,0:T(8,128)(2,1)}, bf16[1,128,128]{2,1,0:T(8,128)(2,1)S(1)}, u32[]{:S(2)}, u32[]{:S(2)}) collective-permute-start(bf16[1,128,128]{2,1,0:T(8,128)(2,1)} %refs_3_.1), channel_id=1, source_target_pairs={{0,1},{1,0},{2,3},{3,2},{4,5},{5,4},{6,7},{7,6},{8,9},{9,8},{10,11... | collective-permute-start | bytes 98312 | tf_op jit(solution)/shard_map/ppermute | solution.py:98
  12.4 8.6 %copy-start.2 = (bf16[1,128,128]{2,1,0:T(8,128)(2,1)}, bf16[1,128,128]{2,1,0:T(8,128)(2,1)S(1)}, u32[]{:S(2)}) copy-start(bf16[1,128,128]{2,1,0:T(8,128)(2,1)S(1)} %collective-permute-done.7.refs_11_) | copy-start | bytes 98308
  12.4 6.9 %collective-permute-start.13 = (bf16[1,128,128]{2,1,0:T(8,128)(2,1)}, bf16[1,128,128]{2,1,0:T(8,128)(2,1)S(1)}, u32[]{:S(2)}, u32[]{:S(2)}) collective-permute-start(bf16[1,128,128]{2,1,0:T(8,128)(2,1)} %refs_3_.1), channel_id=1, source_target_pairs={{0,14},{1,15},{2,12},{3,13},{4,10},{5,11},{6,8},{7,9},{8,6},{9,7},... | collective-permute-start | bytes 98312 | tf_op jit(solution)/shard_map/ppermute | solution.py:98
  13.9 7.1 %copy-start.3 = (bf16[1,128,128]{2,1,0:T(8,128)(2,1)}, bf16[1,128,128]{2,1,0:T(8,128)(2,1)S(1)}, u32[]{:S(2)}) copy-start(bf16[1,128,128]{2,1,0:T(8,128)(2,1)S(1)} %collective-permute-done.5.refs_9_) | copy-start | bytes 98308
  13.9 5.4 %collective-permute-start.12 = (bf16[1,128,128]{2,1,0:T(8,128)(2,1)S(1)}, bf16[1,128,128]{2,1,0:T(8,128)(2,1)S(1)}, u32[]{:S(2)}, u32[]{:S(2)}) collective-permute-start(bf16[1,128,128]{2,1,0:T(8,128)(2,1)S(1)} %collective-permute-done.11.refs_15_), channel_id=1, source_target_pairs={{0,1},{1,0},{2,3},{3,2},{4,5},{5,4},{6,7},{7,6},{8,9},{9,8},{10,11... | collective-permute-start | bytes 98312 | tf_op jit(solution)/shard_map/ppermute | solution.py:98
  13.9 7.1 %copy-start.4 = (bf16[1,128,128]{2,1,0:T(8,128)(2,1)}, bf16[1,128,128]{2,1,0:T(8,128)(2,1)S(1)}, u32[]{:S(2)}) copy-start(bf16[1,128,128]{2,1,0:T(8,128)(2,1)S(1)} %collective-permute-done.3.refs_7_) | copy-start | bytes 98308
  13.9 5.9 %collective-permute-start.10 = (bf16[1,128,128]{2,1,0:T(8,128)(2,1)S(1)}, bf16[1,128,128]{2,1,0:T(8,128)(2,1)S(1)}, u32[]{:S(2)}, u32[]{:S(2)}) collective-permute-start(bf16[1,128,128]{2,1,0:T(8,128)(2,1)S(1)} %collective-permute-done.9.refs_13_), channel_id=1, source_target_pairs={{0,1},{1,0},{2,3},{3,2},{4,5},{5,4},{6,7},{7,6},{8,9},{9,8},{10,11... | collective-permute-start | bytes 98312 | tf_op jit(solution)/shard_map/ppermute | solution.py:98
  15.0 6.1 %copy-start.5 = (bf16[1,128,128]{2,1,0:T(8,128)(2,1)}, bf16[1,128,128]{2,1,0:T(8,128)(2,1)S(1)}, u32[]{:S(2)}) copy-start(bf16[1,128,128]{2,1,0:T(8,128)(2,1)S(1)} %collective-permute-done.1.refs_5_) | copy-start | bytes 98308
  15.0 5.5 %collective-permute-start.8 = (bf16[1,128,128]{2,1,0:T(8,128)(2,1)S(1)}, bf16[1,128,128]{2,1,0:T(8,128)(2,1)S(1)}, u32[]{:S(2)}, u32[]{:S(2)}) collective-permute-start(bf16[1,128,128]{2,1,0:T(8,128)(2,1)S(1)} %collective-permute-done.7.refs_11_), channel_id=1, source_target_pairs={{0,1},{1,0},{2,3},{3,2},{4,5},{5,4},{6,7},{7,6},{8,9},{9,8},{10,11... | collective-permute-start | bytes 98312 | tf_op jit(solution)/shard_map/ppermute | solution.py:98
  15.0 6.1 %copy-start.6 = (bf16[1,128,128]{2,1,0:T(8,128)(2,1)}, bf16[1,128,128]{2,1,0:T(8,128)(2,1)S(1)}, u32[]{:S(2)}) copy-start(bf16[1,128,128]{2,1,0:T(8,128)(2,1)S(1)} %collective-permute-done.refs_4_) | copy-start | bytes 98308
  15.1 5.5 %collective-permute-start.6 = (bf16[1,128,128]{2,1,0:T(8,128)(2,1)S(1)}, bf16[1,128,128]{2,1,0:T(8,128)(2,1)S(1)}, u32[]{:S(2)}, u32[]{:S(2)}) collective-permute-start(bf16[1,128,128]{2,1,0:T(8,128)(2,1)S(1)} %collective-permute-done.5.refs_9_), channel_id=1, source_target_pairs={{0,1},{1,0},{2,3},{3,2},{4,5},{5,4},{6,7},{7,6},{8,9},{9,8},{10,11... | collective-permute-start | bytes 98312 | tf_op jit(solution)/shard_map/ppermute | solution.py:98
  19.3 1.8 %copy-start.7 = (bf16[1,128,128]{2,1,0:T(8,128)(2,1)}, bf16[1,128,128]{2,1,0:T(8,128)(2,1)S(1)}, u32[]{:S(2)}) copy-start(bf16[1,128,128]{2,1,0:T(8,128)(2,1)S(1)} %collective-permute-done.13.refs_17_) | copy-start | bytes 98308
  19.3 1.3 %collective-permute-start.4 = (bf16[1,128,128]{2,1,0:T(8,128)(2,1)S(1)}, bf16[1,128,128]{2,1,0:T(8,128)(2,1)S(1)}, u32[]{:S(2)}, u32[]{:S(2)}) collective-permute-start(bf16[1,128,128]{2,1,0:T(8,128)(2,1)S(1)} %collective-permute-done.3.refs_7_), channel_id=1, source_target_pairs={{0,1},{1,0},{2,3},{3,2},{4,5},{5,4},{6,7},{7,6},{8,9},{9,8},{10,11... | collective-permute-start | bytes 98312 | tf_op jit(solution)/shard_map/ppermute | solution.py:98
  19.3 1.8 %copy-start.8 = (bf16[1,128,128]{2,1,0:T(8,128)(2,1)}, bf16[1,128,128]{2,1,0:T(8,128)(2,1)S(1)}, u32[]{:S(2)}) copy-start(bf16[1,128,128]{2,1,0:T(8,128)(2,1)S(1)} %collective-permute-done.12.refs_16_) | copy-start | bytes 98308
  19.3 1.4 %collective-permute-start.2 = (bf16[1,128,128]{2,1,0:T(8,128)(2,1)S(1)}, bf16[1,128,128]{2,1,0:T(8,128)(2,1)S(1)}, u32[]{:S(2)}, u32[]{:S(2)}) collective-permute-start(bf16[1,128,128]{2,1,0:T(8,128)(2,1)S(1)} %collective-permute-done.1.refs_5_), channel_id=1, source_target_pairs={{0,1},{1,0},{2,3},{3,2},{4,5},{5,4},{6,7},{7,6},{8,9},{9,8},{10,11... | collective-permute-start | bytes 98312 | tf_op jit(solution)/shard_map/ppermute | solution.py:98
  19.8 1.2 %collective-permute-start.14 = (bf16[1,128,128]{2,1,0:T(8,128)(2,1)S(1)}, bf16[1,128,128]{2,1,0:T(8,128)(2,1)S(1)}, u32[]{:S(2)}, u32[]{:S(2)}) collective-permute-start(bf16[1,128,128]{2,1,0:T(8,128)(2,1)S(1)} %collective-permute-done.13.refs_17_), channel_id=1, source_target_pairs={{0,1},{1,0},{2,3},{3,2},{4,5},{5,4},{6,7},{7,6},{8,9},{9,8},{10,11... | collective-permute-start | bytes 98312 | tf_op jit(solution)/shard_map/ppermute | solution.py:98
  34.0 2.1 %collective-permute-start.15 = (f32[8,128,128]{2,1,0:T(8,128)}, f32[8,128,128]{2,1,0:T(8,128)S(1)}, u32[]{:S(2)}, u32[]{:S(2)}) collective-permute-start(f32[8,128,128]{2,1,0:T(8,128)} %get-tuple-element.8), channel_id=1, source_target_pairs={{0,1},{1,0},{2,3},{3,2},{4,5},{5,4},{6,7},{7,6},{8,9},{9,8},{10,11... | collective-permute-start | bytes 1572872 | tf_op jit(solution)/shard_map/ppermute | solution.py:98
  37.3 9.2 %collective-permute-start.16 = (bf16[128,128]{1,0:T(8,128)(2,1)S(1)}, bf16[128,128]{1,0:T(8,128)(2,1)S(1)}, u32[]{:S(2)}, u32[]{:S(2)}) collective-permute-start(bf16[128,128]{1,0:T(8,128)(2,1)S(1)} %get-tuple-element.11), channel_id=1, source_target_pairs={{0,2},{1,3},{2,0},{3,1},{4,6},{5,7},{6,4},{7,5},{8,10},{9,11},{10,... | collective-permute-start | bytes 98312 | tf_op jit(solution)/shard_map/ppermute | solution.py:98
  38.8 8.2 %collective-permute-start.22 = (bf16[128,128]{1,0:T(8,128)(2,1)S(1)}, bf16[128,128]{1,0:T(8,128)(2,1)S(1)}, u32[]{:S(2)}, u32[]{:S(2)}) collective-permute-start(bf16[128,128]{1,0:T(8,128)(2,1)S(1)} %get-tuple-element.12), channel_id=1, source_target_pairs={{0,14},{1,15},{2,12},{3,13},{4,10},{5,11},{6,8},{7,9},{8,6},{9,7},... | collective-permute-start | bytes 98312 | tf_op jit(solution)/shard_map/ppermute | solution.py:98
  41.6 6.8 %collective-permute-start.21 = (bf16[128,128]{1,0:T(8,128)(2,1)S(1)}, bf16[128,128]{1,0:T(8,128)(2,1)S(1)}, u32[]{:S(2)}, u32[]{:S(2)}) collective-permute-start(bf16[128,128]{1,0:T(8,128)(2,1)S(1)} %get-tuple-element.13), channel_id=1, source_target_pairs={{0,12},{1,13},{2,14},{3,15},{4,8},{5,9},{6,10},{7,11},{8,4},{9,5},... | collective-permute-start | bytes 98312 | tf_op jit(solution)/shard_map/ppermute | solution.py:98
  42.6 5.9 %collective-permute-start.20 = (bf16[128,128]{1,0:T(8,128)(2,1)S(1)}, bf16[128,128]{1,0:T(8,128)(2,1)S(1)}, u32[]{:S(2)}, u32[]{:S(2)}) collective-permute-start(bf16[128,128]{1,0:T(8,128)(2,1)S(1)} %get-tuple-element.14), channel_id=1, source_target_pairs={{0,10},{1,11},{2,8},{3,9},{4,14},{5,15},{6,12},{7,13},{8,2},{9,3},... | collective-permute-start | bytes 98312 | tf_op jit(solution)/shard_map/ppermute | solution.py:98
  42.6 6.5 %collective-permute-start.19 = (bf16[128,128]{1,0:T(8,128)(2,1)S(1)}, bf16[128,128]{1,0:T(8,128)(2,1)S(1)}, u32[]{:S(2)}, u32[]{:S(2)}) collective-permute-start(bf16[128,128]{1,0:T(8,128)(2,1)S(1)} %get-tuple-element.15), channel_id=1, source_target_pairs={{0,8},{1,9},{2,10},{3,11},{4,12},{5,13},{6,14},{7,15},{8,0},{9,1},... | collective-permute-start | bytes 98312 | tf_op jit(solution)/shard_map/ppermute | solution.py:98
  46.4 4.8 %collective-permute-start.18 = (bf16[128,128]{1,0:T(8,128)(2,1)S(1)}, bf16[128,128]{1,0:T(8,128)(2,1)S(1)}, u32[]{:S(2)}, u32[]{:S(2)}) collective-permute-start(bf16[128,128]{1,0:T(8,128)(2,1)S(1)} %get-tuple-element.16), channel_id=1, source_target_pairs={{0,6},{1,7},{2,4},{3,5},{4,2},{5,3},{6,0},{7,1},{8,14},{9,15},{10,... | collective-permute-start | bytes 98312 | tf_op jit(solution)/shard_map/ppermute | solution.py:98
  46.9 4.3 %collective-permute-start.17 = (bf16[128,128]{1,0:T(8,128)(2,1)S(1)}, bf16[128,128]{1,0:T(8,128)(2,1)S(1)}, u32[]{:S(2)}, u32[]{:S(2)}) collective-permute-start(bf16[128,128]{1,0:T(8,128)(2,1)S(1)} %get-tuple-element.17), channel_id=1, source_target_pairs={{0,4},{1,5},{2,6},{3,7},{4,0},{5,1},{6,2},{7,3},{8,12},{9,13},{10,... | collective-permute-start | bytes 98312 | tf_op jit(solution)/shard_map/ppermute | solution.py:98
  (6 other events, 4.3 us)

commit v2 on v1

--- a/solution.py
+++ b/solution.py
@@ -14,61 +14,60 @@
     )
 
 
-def table_kernel(nsec, nops, me_ref, live_ref, coup_ref, *refs):
-    psi = refs[:nsec]
-    left_ref, right_ref = refs[nsec : nsec + 2]
-    odd_ref, even_ref = refs[nsec + 2 : nsec + 4]
-    half_ref, sum_ref = refs[nsec + 4 :]
-    m = left_ref.shape[1]
+def table_kernel(
+    me_ref, live_ref, coup_ref, mine_ref, other_ref, left_ref, right_ref,
+    sums_ref, sums_other_ref, half_ref, sum_ref,
+):
+    nops, m, _ = left_ref.shape
+    chips = mine_ref.shape[0]
     me = me_ref[0]
 
+    def place(sector):
+        return ((sector ^ me) & 1) * chips + (sector >> 1)
+
     step = 4
-    for s in range(0, nsec, 2):
-        pair = jnp.concatenate([psi[s][0], psi[s + 1][0]], axis=1)
+    for s in range(0, 2 * chips, 2):
+        psi_ref = mine_ref if s < chips else other_ref
+        pair = jnp.concatenate([psi_ref[s % chips], psi_ref[s % chips + 1]], axis=1)
         for g in range(0, nops, step):
             rows = left_ref[g : g + step].reshape(step * m, m)
             both = jnp.dot(rows, pair, preferred_element_type=jnp.float32).astype(jnp.bfloat16)
             half_ref[s, g : g + step] = both[:, :m].reshape(step, m, m)
             half_ref[s + 1, g : g + step] = both[:, m:].reshape(step, m, m)
 
-    @pl.loop(0, nsec)
+    @pl.loop(0, 2 * chips)
     def _(t):
         sum_ref[t] = jnp.zeros(sum_ref.shape[1:], jnp.float32)
 
     @pl.loop(0, live_ref[0])
     def _(c):
         g = coup_ref[0, c]
-        s = coup_ref[1, c] ^ me
-        t = coup_ref[2, c] ^ me
-        sum_ref[t, g] += half_ref[s, g].astype(jnp.float32)
+        sum_ref[place(coup_ref[2, c]), g] += half_ref[place(coup_ref[1, c]), g].astype(jnp.float32)
 
     rights = jnp.concatenate([right_ref[g] for g in range(nops)], axis=1)
-    for t in range(nsec):
+    for t in range(2 * chips):
         sums = jnp.concatenate([sum_ref[t, g].astype(jnp.bfloat16) for g in range(nops)], axis=1)
-        out = transposed_dot(sums, rights)
-        if t % 2:
-            odd_ref[t // 2] = out
-        else:
-            even_ref[t // 2] = out
+        out_ref = sums_ref if t < chips else sums_other_ref
+        out_ref[t % chips] = transposed_dot(sums, rights)
 
 
-def by_table(psi_blocks, left_ops, right_ops, couplings, live, me):
-    nsec = len(psi_blocks)
+def by_table(mine, other, left_ops, right_ops, couplings, live, me):
+    chips = mine.shape[0]
     nops, m, _ = left_ops.shape
     vmem = pl.BlockSpec(memory_space=pltpu.VMEM)
     smem = pl.BlockSpec(memory_space=pltpu.SMEM)
     return pl.pallas_call(
-        lambda *refs: table_kernel(nsec, nops, *refs),
-        out_shape=[jax.ShapeDtypeStruct((nsec // 2, m, m), jnp.float32)] * 2,
-        in_specs=[smem] * 3 + [vmem] * (nsec + 2),
+        table_kernel,
+        out_shape=[jax.ShapeDtypeStruct((chips, m, m), jnp.float32)] * 2,
+        in_specs=[smem] * 3 + [vmem] * 4,
         out_specs=[vmem] * 2,
         scratch_shapes=[
-            pltpu.VMEM((nsec, nops, m, m), jnp.bfloat16),
-            pltpu.VMEM((nsec, nops, m, m), jnp.float32),
+            pltpu.VMEM((2 * chips, nops, m, m), jnp.bfloat16),
+            pltpu.VMEM((2 * chips, nops, m, m), jnp.float32),
         ],
         compiler_params=pltpu.CompilerParams(vmem_limit_bytes=VMEM_LIMIT),
         name="table",
-    )(me, live, couplings, *psi_blocks, left_ops, right_ops)
+    )(me, live, couplings, mine, other, left_ops, right_ops)
 
 
 def slot_kernel(live_ref, coup_ref, psi_ref, left_ref, right_ref, out_ref):
@@ -100,18 +99,17 @@
 
 def shards_small(ops, psi, left_ops, right_ops, couplings, live):
     me = lax.axis_index("ops").astype(jnp.int32)
-    blocks = [None] * ops
-    blocks[0] = psi
-    for d in range(2, ops, 2):
-        blocks[d] = swap(psi, ops, d)
-    for d in range(0, ops, 2):
-        blocks[d + 1] = swap(blocks[d], ops, 1)
-    odd, even = by_table(blocks, left_ops, right_ops, couplings, live, me[None])
-    chip = even + swap(odd, ops, 1)
-    total = chip[0]
-    for d in range(2, ops, 2):
-        total = total + swap(chip[d // 2].astype(jnp.bfloat16), ops, d).astype(jnp.float32)
-    return total[None]
+    same_core = [list(range(core, ops, 2)) for core in range(2)]
+    copies = jnp.broadcast_to(psi, (ops // 2, *psi.shape[1:]))
+    mine = lax.all_to_all(copies, "ops", 0, 0, axis_index_groups=same_core, tiled=True)
+    other = swap(mine, ops, 1)
+    sums, sums_other = by_table(mine, other, left_ops, right_ops, couplings, live, me[None])
+    chip = sums + swap(sums_other, ops, 1)
+    parts = lax.all_to_all(
+        chip.astype(jnp.bfloat16), "ops", 0, 0, axis_index_groups=same_core, tiled=True
+    )
+    own = (jnp.arange(ops // 2, dtype=jnp.int32) == me >> 1)[:, None, None]
+    return jnp.sum(jnp.where(own, chip, parts.astype(jnp.float32)), axis=0, keepdims=True)
 
 
 def shards_large(psi, left_ops, right_ops, couplings, live):

time: 52.3 us -> 51.1 us (0.977)
  starting transfers between devices: 26.3 us -> 3.42 us
  blocking collectives: 0 us -> 16 us
  waiting for transfers between devices: 10.1 us -> 12.4 us
  Pallas kernels: 12.3 us -> 13.8 us
  local copies, waits for them, and re-layouts: 0.6 us -> 1.49 us
  other arithmetic: 1.78 us -> 2.57 us
    ppermute x23 -> x2, starting transfers between devices: 26.3 us -> 0.01 us  [swap(): return lax.ppermute(x, 'ops', [(i, i ^ d) for i in range(ops)])]
    all_to_all x0 -> x1, blocking collectives: none -> 16 us  [shards_small(): lax.all_to_all(copies, 'ops', 0, 0, axis_index_groups=same_core, tiled=True)]
    all_to_all x0 -> x1, waiting for transfers between devices: none -> 9.42 us  [shards_small(): lax.all_to_all(chip.astype(jnp.bfloat16), 'ops', 0, 0, axis_index_groups=...]
    ppermute x23 -> x2, waiting for transfers between devices: 10.1 us -> 3 us  [swap(): return lax.ppermute(x, 'ops', [(i, i ^ d) for i in range(ops)])]
    all_to_all x0 -> x1, starting transfers between devices: none -> 3.41 us  [shards_small(): lax.all_to_all(chip.astype(jnp.bfloat16), 'ops', 0, 0, axis_index_groups=...]
    convert_element_type x0 -> x1, other arithmetic: none -> 1.81 us  [shards_small(): chip.astype(jnp.bfloat16)]
    pallas_call x1, Pallas kernels: 12.3 us -> 13.8 us  [by_table(): pl.pallas_call(table_kernel, out_shape=[jax.ShapeDtypeStruct((chips, m, m...]
    another operation x1 -> x0, other arithmetic: 1.12 us -> none
  transfers between devices with their start and end apart: 23 -> 3, of which waited for: 8 -> 3; matrix products, arithmetic and copies ran while one was open for 0% -> 0% of each run, Pallas kernels for 0% -> 0%
where the time goes in v2:
time: 51.1 us; the launch traced here: 50.4 us
  blocking collectives  16 us (31%)
  Pallas kernels  13.8 us (27%)
  waiting for transfers between devices  12.4 us (24%)
  starting transfers between devices  3.42 us (7%)
  other arithmetic  2.57 us (5%)
  local copies, waits for them, and re-layouts  1.49 us (3%)
  between operations  0.68 us (1%)
    all_to_all x1, blocking collectives, shards_small(): lax.all_to_all(copies, 'ops', 0, 0, axis_index_groups=same_core, tiled=True)  16 us
    pallas_call x1, Pallas kernels, by_table(): pl.pallas_call(table_kernel, out_shape=[jax.ShapeDtypeStruct((chips, m, m...  13.8 us
    all_to_all x1, waiting for transfers between devices, shards_small(): lax.all_to_all(chip.astype(jnp.bfloat16), 'ops', 0, 0, axis_index_groups=...  9.42 us
    all_to_all x1, starting transfers between devices, shards_small(): lax.all_to_all(chip.astype(jnp.bfloat16), 'ops', 0, 0, axis_index_groups=...  3.41 us
    ppermute x2, waiting for transfers between devices, swap(): return lax.ppermute(x, 'ops', [(i, i ^ d) for i in range(ops)])  3 us
    convert_element_type x1, other arithmetic, shards_small(): chip.astype(jnp.bfloat16)  1.81 us
  transfers between devices with their start and end apart: 3, of which 3 were waited for; matrix products, arithmetic and copies ran while one was open for 0% of the time, Pallas kernels for 0%

profile of v2, /device:TPU:0, one launch (start us, length us, event | category | flops | bytes accessed | tf_op | source)
XLA Modules:
  0.0 50.4 jit_solution(16391384123507318242)
XLA Ops:
  0.0 0.8 %broadcast_in_dim.25 = bf16[8,128,128]{2,1,0:T(8,128)(2,1)S(1)} broadcast(bf16[128,128]{1,0:T(8,128)(2,1)} %bitcast.3), dimensions={1,2} | broadcast | bytes 294912 | tf_op jit(solution)/shard_map/broadcast_in_dim | solution.py:103
  0.8 16.0 %all_to_all.10.mine_ref = bf16[8,128,128]{2,1,0:T(8,128)(2,1)S(1)} all-to-all(bf16[8,128,128]{2,1,0:T(8,128)(2,1)S(1)} %broadcast_in_dim.25), channel_id=1, replica_groups={{0,2,4,6,8,10,12,14},{1,3,5,7,9,11,13,15},{16,18,20,22,24,26,28,30},{17..., dimensions={0} | all-to-all | bytes 524288 | tf_op jit(solution)/shard_map/all_to_all | solution.py:104
  16.8 0.0 copy-start
  16.8 0.0 collective-permute-start
  17.4 0.9 %collective-permute-done.other_ref = bf16[8,128,128]{2,1,0:T(8,128)(2,1)S(1)} collective-permute-done((bf16[8,128,128]{2,1,0:T(8,128)(2,1)S(1)}, bf16[8,128,128]{2,1,0:T(8,128)(2,1)S(1)}, u32[]{:S(2)}, u32[]{:S(2)}) %collective-permute-start) | collective-permute-done | bytes 262176 | tf_op jit(solution)/shard_map/ppermute | solution.py:97
  18.3 0.0 copy-start.1
  18.3 0.0 copy-done
  18.3 0.7 %copy-done.1 = bf16[8,128,128]{2,1,0:T(8,128)(2,1)} copy-done((bf16[8,128,128]{2,1,0:T(8,128)(2,1)}, bf16[8,128,128]{2,1,0:T(8,128)(2,1)S(1)}, u32[]{:S(2)}) %copy-start.1) | copy-done | bytes 262168
  19.0 13.8 %table.1 = (f32[8,128,128]{2,1,0:T(8,128)}, f32[8,128,128]{2,1,0:T(8,128)}) custom-call(s32[1]{0:T(128)} %bitcast.me_ref, s32[1]{0:T(128)S(6)} %copy.6.live_ref, s32[3,384]{1,0:T(4,128)} %coup_ref.1, bf16[8,128,128]{2,1,0:T(8,128)(2,1)} %copy-done, bf16[8,128,128]{2,1,0:T(8,128)(2,1)} %copy-done.1, bf16[16,128,128]{2,1,0:T(8,128)(2,1)} %left_ref.1, ...), custom_call_target="tpu_custom_call" | custom-call | tf_op jit(solution)/shard_map/table/pallas_call | solution.py:59
  32.8 0.0 collective-permute-start.1
  32.8 2.1 %collective-permute-done.1 = f32[8,128,128]{2,1,0:T(8,128)S(1)} collective-permute-done((f32[8,128,128]{2,1,0:T(8,128)}, f32[8,128,128]{2,1,0:T(8,128)S(1)}, u32[]{:S(2)}, u32[]{:S(2)}) %collective-permute-start.1) | collective-permute-done | bytes 524320 | tf_op jit(solution)/shard_map/ppermute | solution.py:97
  34.9 1.8 %fusion = (bf16[8,128,128]{2,1,0:T(8,128)(2,1)}, f32[8,128,128]{2,1,0:T(8,128)S(1)}) fusion(f32[8,128,128]{2,1,0:T(8,128)} %get-tuple-element.7, f32[8,128,128]{2,1,0:T(8,128)S(1)} %collective-permute-done.1), kind=kLoop, calls=%fused_computation.2 | loop fusion | flops 262144 | bytes 1835008 | tf_op jit(solution)/shard_map/convert_element_type | solution.py:109
  36.8 3.4 %all-to-all-start.1 = ((bf16[8,128,128]{2,1,0:T(8,128)(2,1)}), bf16[8,128,128]{2,1,0:T(8,128)(2,1)S(1)}, u32[]{:S(2)}, u32[]{:S(2)}) async-start(bf16[8,128,128]{2,1,0:T(8,128)(2,1)} %get-tuple-element.9), calls=%async_computation.1 | async-start | bytes 524288 | tf_op jit(solution)/shard_map/all_to_all | solution.py:108
  40.2 9.4 %all-to-all-done.1 = bf16[8,128,128]{2,1,0:T(8,128)(2,1)S(1)} async-done(((bf16[8,128,128]{2,1,0:T(8,128)(2,1)}), bf16[8,128,128]{2,1,0:T(8,128)(2,1)S(1)}, u32[]{:S(2)}, u32[]{:S(2)}) %all-to-all-start.1) | async-done | bytes 262176 | tf_op jit(solution)/shard_map/all_to_all | solution.py:108
  49.6 0.7 %select_reduce_fusion = f32[128,128]{1,0:T(8,128)} fusion(f32[8,128,128]{2,1,0:T(8,128)S(1)} %get-tuple-element.10, bf16[8,128,128]{2,1,0:T(8,128)(2,1)S(1)} %all-to-all-done.1, pred[8]{0:T(512)(128)(4,1)S(1)} %iota_compare_fusion), kind=kLoop, calls=%fused_computation | loop fusion | flops 376832 | bytes 851976 | tf_op jit(solution)/shard_map/reduce_sum | solution.py:112
  (1 shorter events, 0.0 us)
Async XLA Ops:
  16.8 1.5 %copy-start = (bf16[8,128,128]{2,1,0:T(8,128)(2,1)}, bf16[8,128,128]{2,1,0:T(8,128)(2,1)S(1)}, u32[]{:S(2)}) copy-start(bf16[8,128,128]{2,1,0:T(8,128)(2,1)S(1)} %all_to_all.10.mine_ref) | copy-start | bytes 786436
  16.8 1.5 %collective-permute-start = (bf16[8,128,128]{2,1,0:T(8,128)(2,1)S(1)}, bf16[8,128,128]{2,1,0:T(8,128)(2,1)S(1)}, u32[]{:S(2)}, u32[]{:S(2)}) collective-permute-start(bf16[8,128,128]{2,1,0:T(8,128)(2,1)S(1)} %all_to_all.10.mine_ref), channel_id=1, source_target_pairs={{0,1},{1,0},{2,3},{3,2},{4,5},{5,4},{6,7},{7,6},{8,9},{9,8},{10,11... | collective-permute-start | bytes 786440 | tf_op jit(solution)/shard_map/ppermute | solution.py:97
  18.3 0.7 %copy-start.1 = (bf16[8,128,128]{2,1,0:T(8,128)(2,1)}, bf16[8,128,128]{2,1,0:T(8,128)(2,1)S(1)}, u32[]{:S(2)}) copy-start(bf16[8,128,128]{2,1,0:T(8,128)(2,1)S(1)} %collective-permute-done.other_ref) | copy-start | bytes 786436
  32.8 2.1 %collective-permute-start.1 = (f32[8,128,128]{2,1,0:T(8,128)}, f32[8,128,128]{2,1,0:T(8,128)S(1)}, u32[]{:S(2)}, u32[]{:S(2)}) collective-permute-start(f32[8,128,128]{2,1,0:T(8,128)} %get-tuple-element.8), channel_id=1, source_target_pairs={{0,1},{1,0},{2,3},{3,2},{4,5},{5,4},{6,7},{7,6},{8,9},{9,8},{10,11... | collective-permute-start | bytes 1572872 | tf_op jit(solution)/shard_map/ppermute | solution.py:97
  36.8 12.9 %all-to-all-start.1 = ((bf16[8,128,128]{2,1,0:T(8,128)(2,1)}), bf16[8,128,128]{2,1,0:T(8,128)(2,1)S(1)}, u32[]{:S(2)}, u32[]{:S(2)}) async-start(bf16[8,128,128]{2,1,0:T(8,128)(2,1)} %get-tuple-element.9), calls=%async_computation.1 | async-start | bytes 524288 | tf_op jit(solution)/shard_map/all_to_all | solution.py:108

commit v3 on v2

v3 whole, which is shorter than its diff:
```python
import jax
import jax.numpy as jnp
from jax import lax
from jax.experimental import pallas as pl
from jax.experimental.pallas import tpu as pltpu
from jax.sharding import PartitionSpec as P

VMEM = pl.BlockSpec(memory_space=pltpu.VMEM)
SMEM = pl.BlockSpec(memory_space=pltpu.SMEM)

BLOCKS, CELL_BLOCK, SUM_FIRST, SUM_COUNT, TOTALS = range(5)


def transposed_dot(a, b):
    return lax.dot_general(
        a, b, (((1,), (1,)), ((), ())), preferred_element_type=jnp.float32
    )


def iota(shape, axis):
    return lax.broadcasted_iota(jnp.int32, shape, axis)


def count(mask, axis):
    return jnp.sum(mask.astype(jnp.float32), axis=axis, keepdims=True).astype(jnp.int32)


def picked(mask, values, axis):
    kept = jnp.where(mask, values, 0).astype(jnp.float32)
    return jnp.sum(kept, axis=axis, keepdims=True).astype(jnp.int32)


def as_column(row):
    n = row.shape[1]
    return picked(iota((n, n), 0) == iota((n, n), 1), row, 1)


def order_kernel(bits, nops, me_ref, live_ref, coup_ref, out_ref):
    slots = coup_ref.shape[1]
    cells = (1 << bits) * nops
    me = me_ref[0]

    def place(sector):
        near = sector ^ me
        spot = near & 0
        for b in range(bits):
            spot = spot | (((near >> b) & 1) << (bits - 1 - b))
        return spot

    g = coup_ref[0:1, :]
    alive = iota((1, slots), 1) < live_ref[0]
    cell = jnp.where(alive, place(coup_ref[2:3, :]) * nops + g, cells)
    block = place(coup_ref[1:2, :]) * nops + g
    cell_col = as_column(cell)
    block_col = as_column(block)
    square = (slots, slots)
    ahead = (cell < cell_col) | ((cell == cell_col) & (iota(square, 1) < iota(square, 0)))
    spot_col = count(ahead, 1)
    out_ref[BLOCKS : BLOCKS + 1, :] = picked(spot_col == iota(square, 1), block_col, 0)

    lane = iota((1, cells), 1)
    first = count(cell_col < lane, 0)
    here = cell_col == lane
    number = count(here, 0)
    only = picked(here, block_col, 0)
    kind = (number > 1).astype(jnp.int32) + (number > 2) + (number > 4)
    square = (cells, cells)
    kind_col = as_column(kind)
    ahead = (kind_col > kind) | ((kind_col == kind) & (iota(square, 0) < iota(square, 1)))
    spot = count(ahead, 0)
    cell_block = jnp.where(number == 0, cells, jnp.where(number == 1, only, cells + 1 + spot))
    chosen = as_column(spot) == iota(square, 1)
    out_ref[CELL_BLOCK : CELL_BLOCK + 1, :cells] = cell_block
    out_ref[SUM_FIRST : SUM_FIRST + 1, :cells] = picked(chosen, as_column(first), 0)
    out_ref[SUM_COUNT : SUM_COUNT + 1, :cells] = picked(chosen, as_column(number), 0)
    small = iota((1, 128), 1)
    ends = [count(kind > k, 1) for k in (2, 1, 0)]
    out_ref[TOTALS : TOTALS + 1, :128] = jnp.where(
        small == 0, ends[0], jnp.where(small == 1, ends[1], ends[2])
    )


def order_slots(bits, nops, couplings, live, me):
    slots = couplings.shape[1]
    cells = (1 << bits) * nops
    return pl.pallas_call(
        lambda *refs: order_kernel(bits, nops, *refs),
        out_shape=jax.ShapeDtypeStruct((8, max(slots, cells)), jnp.int32),
        in_specs=[SMEM, SMEM, VMEM],
        out_specs=VMEM,
        compiler_params=pltpu.CompilerParams(vmem_limit_bytes=16 * 1024 * 1024),
        cost_estimate=pl.CostEstimate(
            flops=20 * slots * slots, bytes_accessed=4 * 11 * slots, transcendentals=0
        ),
        name="order",
    )(me, live, couplings)


def table_kernel(order_ref, near_ref, far_ref, left_ref, right_ref, keep_ref, send_ref, block_ref):
    nops, m, _ = left_ref.shape
    half = near_ref.shape[0]
    cells = 2 * half * nops

    step = 4
    for s in range(0, 2 * half, 2):
        psi_ref = near_ref if s < half else far_ref
        pair = jnp.concatenate([psi_ref[s % half], psi_ref[s % half + 1]], axis=1)
        for g in range(0, nops, step):
            rows = left_ref[g : g + step].reshape(step * m, m)
            both = jnp.dot(rows, pair, preferred_element_type=jnp.float32).astype(jnp.bfloat16)
            at = s * nops + g
            block_ref[at : at + step] = both[:, :m].reshape(step, m, m)
            block_ref[at + nops : at + nops + step] = both[:, m:].reshape(step, m, m)
    block_ref[cells] = jnp.zeros((m, m), jnp.bfloat16)

    many, some, two = (order_ref[TOTALS, k] for k in range(3))

    @pl.loop(0, many)
    def _(k):
        first = order_ref[SUM_FIRST, k]

        def add(j, total):
            return total + block_ref[order_ref[BLOCKS, first + j]].astype(jnp.float32)

        total = lax.fori_loop(0, order_ref[SUM_COUNT, k], add, jnp.zeros((m, m), jnp.float32))
        block_ref[cells + 1 + k] = total.astype(jnp.bfloat16)

    @pl.loop(many, some)
    def _(k):
        first = order_ref[SUM_FIRST, k]
        fourth = jnp.where(order_ref[SUM_COUNT, k] == 4, order_ref[BLOCKS, first + 3], cells)
        total = block_ref[order_ref[BLOCKS, first]].astype(jnp.float32)
        total += block_ref[order_ref[BLOCKS, first + 1]].astype(jnp.float32)
        total += block_ref[order_ref[BLOCKS, first + 2]].astype(jnp.float32)
        total += block_ref[fourth].astype(jnp.float32)
        block_ref[cells + 1 + k] = total.astype(jnp.bfloat16)

    @pl.loop(some, two, step=2)
    def _(k):
        ks = (k, jnp.minimum(k + 1, two - 1))
        firsts = [order_ref[SUM_FIRST, k] for k in ks]
        totals = [
            block_ref[order_ref[BLOCKS, first]] + block_ref[order_ref[BLOCKS, first + 1]]
            for first in firsts
        ]
        for k, total in zip(ks, totals):
            block_ref[cells + 1 + k] = total

    rights = jnp.concatenate([right_ref[g] for g in range(nops)], axis=1)
    for t in range(0, 2 * half, 2):
        rows = [
            jnp.concatenate(
                [block_ref[order_ref[CELL_BLOCK, (t + i) * nops + g]] for g in range(nops)], axis=1
            )
            for i in range(2)
        ]
        out = transposed_dot(jnp.concatenate(rows, axis=0), rights)
        out_ref = keep_ref if t < half else send_ref
        out_ref[t % half : t % half + 2] = out.reshape(2, m, m)


def by_table(near, far, left_ops, right_ops, order):
    half = near.shape[0]
    nops, m, _ = left_ops.shape
    cells = 2 * half * nops
    slots = order.shape[1]
    return pl.pallas_call(
        table_kernel,
        out_shape=[jax.ShapeDtypeStruct((half, m, m), jnp.float32)] * 2,
        in_specs=[SMEM] + [VMEM] * 4,
        out_specs=[VMEM] * 2,
        scratch_shapes=[pltpu.VMEM((cells + 1 + slots // 2, m, m), jnp.bfloat16)],
        compiler_params=pltpu.CompilerParams(vmem_limit_bytes=24 * 1024 * 1024),
        cost_estimate=pl.CostEstimate(
            flops=4 * cells * m**3, bytes_accessed=4 * nops * m * m, transcendentals=0
        ),
        name="table",
    )(order, near, far, left_ops, right_ops)


def slot_kernel(live_ref, coup_ref, psi_ref, left_ref, right_ref, out_ref):
    out_ref[...] = jnp.zeros_like(out_ref)

    @pl.loop(0, live_ref[0])
    def _(c):
        g = coup_ref[0, c]
        half = jnp.dot(left_ref[g], psi_ref[coup_ref[1, c]], preferred_element_type=jnp.float32)
        out_ref[coup_ref[2, c]] += transposed_dot(half.astype(jnp.bfloat16), right_ref[g])


def by_slot(whole, left_ops, right_ops, couplings, live):
    return pl.pallas_call(
        slot_kernel,
        out_shape=jax.ShapeDtypeStruct(whole.shape, jnp.float32),
        in_specs=[SMEM] * 2 + [VMEM] * 3,
        out_specs=VMEM,
        compiler_params=pltpu.CompilerParams(vmem_limit_bytes=60 * 1024 * 1024),
        name="slots",
    )(live, couplings, whole, left_ops, right_ops)


def swap(x, ops, d):
    return lax.ppermute(x, "ops", [(i, i ^ d) for i in range(ops)])


def shards_small(ops, psi, left_ops, right_ops, couplings, live):
    bits = ops.bit_length() - 1
    me = lax.axis_index("ops").astype(jnp.int32)
    order = order_slots(bits, left_ops.shape[0], couplings, live, me[None])
    near = psi
    for b in reversed(range(1, bits)):
        near = jnp.concatenate([near, swap(near, ops, 1 << b)], axis=0)
    far = swap(near, ops, 1)
    keep, send = by_table(near, far, left_ops, right_ops, order)
    for b in range(bits):
        came = swap(send, ops, 1 << b).astype(jnp.float32)
        half = keep.shape[0] // 2
        if half:
            send = (keep[half:] + came[half:]).astype(jnp.bfloat16)
            keep = keep[:half] + came[:half]
    return keep + came


def shards_large(psi, left_ops, right_ops, couplings, live):
    whole = lax.all_gather(psi, "ops", axis=0, tiled=True)
    total = by_slot(whole, left_ops, right_ops, couplings, live)
    return lax.psum_scatter(total, "ops", scatter_dimension=0, tiled=True)


def solution(mesh):
    ops = mesh.shape["ops"]
    placed = (
        P(("groups", "ops"), None, None),
        P(("groups", "ops"), None, None),
        P(("groups", "ops"), None, None),
        P(None, ("groups", "ops")),
        P(("groups", "ops")),
    )

    def shards(psi, *rest):
        small = psi.shape[0] == 1 and 4 <= ops <= 16 and ops & (ops - 1) == 0
        if small:
            return shards_small(ops, psi, *rest)
        return shards_large(psi, *rest)

    return jax.shard_map(
        shards,
        mesh=mesh,
        in_specs=placed,
        out_specs=P(("groups", "ops"), None, None),
        check_vma=False,
    )
```

time: 51.1 us -> 45.3 us (0.89)
  blocking collectives: 16 us -> 0 us
  starting transfers between devices: 3.42 us -> 15 us
  waiting for transfers between devices: 12.4 us -> 19.8 us
  Pallas kernels: 13.8 us -> 6.46 us
  other arithmetic: 2.57 us -> 1.56 us
    ppermute x2 -> x8, waiting for transfers between devices: 3 us -> 19.8 us  [swap(): return lax.ppermute(x, 'ops', [(i, i ^ d) for i in range(ops)])]
    all_to_all x1 -> x0, blocking collectives: 16 us -> none  [shards_small(): lax.all_to_all(copies, 'ops', 0, 0, axis_index_groups=same_core, tiled=True)]
    ppermute x2 -> x8, starting transfers between devices: 0.01 us -> 15 us  [swap(): return lax.ppermute(x, 'ops', [(i, i ^ d) for i in range(ops)])]
    all_to_all x1 -> x0, waiting for transfers between devices: 9.42 us -> none  [shards_small(): lax.all_to_all(chip.astype(jnp.bfloat16), 'ops', 0, 0, axis_index_groups=...]
    pallas_call x1 -> x2, Pallas kernels: 13.8 us -> 6.46 us  [the longest x1 5.85 us: by_table(): pl.pallas_call(table_kernel, out_shape=[jax.ShapeDtypeStruct((half, m, m)...]
    all_to_all x1 -> x0, starting transfers between devices: 3.41 us -> none  [shards_small(): lax.all_to_all(chip.astype(jnp.bfloat16), 'ops', 0, 0, axis_index_groups=...]
    convert_element_type x1 -> x3, other arithmetic: 1.81 us -> 0.04 us  [the longest x2 0.03 us: shards_small(): came = swap(send, ops, 1 << b).astype(jnp.float32)]
    broadcast_in_dim x1 -> x0, local copies, waits for them, and re-layouts: 0.79 us -> none  [shards_small(): copies = jnp.broadcast_to(psi, (ops // 2, *psi.shape[1:]))]
  transfers between devices with their start and end apart: 3 -> 8, of which waited for: 3 -> 8; matrix products, arithmetic and copies ran while one was open for 0% -> 0% of each run, Pallas kernels for 0% -> 1%
where the time goes in v3:
time: 45.3 us; the launch traced here: 44.7 us
  waiting for transfers between devices  19.8 us (44%)
  starting transfers between devices  15 us (33%)
  Pallas kernels  6.46 us (14%)
  other arithmetic  1.56 us (3%)
  local copies, waits for them, and re-layouts  1.1 us (2%)
  between operations  0.73 us (2%)
    ppermute x8, waiting for transfers between devices, swap(): return lax.ppermute(x, 'ops', [(i, i ^ d) for i in range(ops)])  19.8 us
    ppermute x8, starting transfers between devices, swap(): return lax.ppermute(x, 'ops', [(i, i ^ d) for i in range(ops)])  15 us
    pallas_call x1, Pallas kernels, by_table(): pl.pallas_call(table_kernel, out_shape=[jax.ShapeDtypeStruct((half, m, m)...  5.85 us
    unnamed x11, local copies, waits for them, and re-layouts  1.08 us
  transfers between devices with their start and end apart: 8, of which 8 were waited for; matrix products, arithmetic and copies ran while one was open for 0% of the time, Pallas kernels for 1%

profile of v3, /device:TPU:0, one launch (start us, length us, event | category | flops | bytes accessed | tf_op | source)
XLA Modules:
  0.0 44.7 jit_solution(583252595724633597)
XLA Ops:
  0.0 0.0 copy-start.3
  0.0 0.0 copy-start.1
  0.0 4.0 %collective-permute-start = (bf16[1,128,128]{2,1,0:T(8,128)(2,1)}, bf16[1,128,128]{2,1,0:T(8,128)(2,1)S(1)}, u32[]{:S(2)}, u32[]{:S(2)}) collective-permute-start(bf16[1,128,128]{2,1,0:T(8,128)(2,1)} %param.5), channel_id=1, source_target_pairs={{0,8},{1,9},{2,10},{3,11},{4,12},{5,13},{6,14},{7,15},{8,0},{9,1},... | collective-permute-start | bytes 98312 | tf_op jit(solution)/shard_map/ppermute | solution.py:203
  4.0 2.5 %collective-permute-done = bf16[1,128,128]{2,1,0:T(8,128)(2,1)S(1)} collective-permute-done((bf16[1,128,128]{2,1,0:T(8,128)(2,1)}, bf16[1,128,128]{2,1,0:T(8,128)(2,1)S(1)}, u32[]{:S(2)}, u32[]{:S(2)}) %collective-permute-start) | collective-permute-done | bytes 32800 | tf_op jit(solution)/shard_map/ppermute | solution.py:203
  6.6 0.8 %pad_maximum_fusion.1 = bf16[2,128,128]{2,1,0:T(8,128)(2,1)S(1)} fusion(bf16[1,128,128]{2,1,0:T(8,128)(2,1)S(1)} %collective-permute-done, bf16[1,128,128]{2,1,0:T(8,128)(2,1)} %param.5), kind=kLoop, calls=%fused_computation.11 | loop fusion | flops 32768 | bytes 131072 | tf_op jit(solution)/shard_map/concatenate | solution.py:212
  7.3 1.5 %collective-permute-start.1 = (bf16[2,128,128]{2,1,0:T(8,128)(2,1)S(1)}, bf16[2,128,128]{2,1,0:T(8,128)(2,1)S(1)}, u32[]{:S(2)}, u32[]{:S(2)}) collective-permute-start(bf16[2,128,128]{2,1,0:T(8,128)(2,1)S(1)} %pad_maximum_fusion.1), channel_id=1, source_target_pairs={{0,4},{1,5},{2,6},{3,7},{4,0},{5,1},{6,2},{7,3},{8,12},{9,13},{10,... | collective-permute-start | bytes 196616 | tf_op jit(solution)/shard_map/ppermute | solution.py:203
  8.8 0.0 copy-done.3
  8.8 2.8 %collective-permute-done.1 = bf16[2,128,128]{2,1,0:T(8,128)(2,1)S(1)} collective-permute-done((bf16[2,128,128]{2,1,0:T(8,128)(2,1)S(1)}, bf16[2,128,128]{2,1,0:T(8,128)(2,1)S(1)}, u32[]{:S(2)}, u32[]{:S(2)}) %collective-permute-start.1) | collective-permute-done | bytes 65568 | tf_op jit(solution)/shard_map/ppermute | solution.py:203
  11.6 1.7 %collective-permute-start.2 = (bf16[4,128,128]{2,1,0:T(8,128)(2,1)S(1)}, bf16[4,128,128]{2,1,0:T(8,128)(2,1)S(1)}, u32[]{:S(2)}, u32[]{:S(2)}) collective-permute-start(bf16[4,128,128]{2,1,0:T(8,128)(2,1)S(1)} %pad_maximum_fusion), channel_id=1, source_target_pairs={{0,2},{1,3},{2,0},{3,1},{4,6},{5,7},{6,4},{7,5},{8,10},{9,11},{10,... | collective-permute-start | bytes 393224 | tf_op jit(solution)/shard_map/ppermute | solution.py:203
  13.4 3.3 %collective-permute-done.2 = bf16[4,128,128]{2,1,0:T(8,128)(2,1)S(1)} collective-permute-done((bf16[4,128,128]{2,1,0:T(8,128)(2,1)S(1)}, bf16[4,128,128]{2,1,0:T(8,128)(2,1)S(1)}, u32[]{:S(2)}, u32[]{:S(2)}) %collective-permute-start.2) | collective-permute-done | bytes 131104 | tf_op jit(solution)/shard_map/ppermute | solution.py:203
  16.7 0.0 copy-start
  16.7 0.1 collective-permute-start.3
  17.4 0.0 copy-done
  17.4 0.6 %order.1.order_ref = s32[8,384]{1,0:T(8,128)S(1)} custom-call(s32[1]{0:T(128)} %bitcast.refs_0_, s32[1]{0:T(128)S(6)} %copy.9.refs_1_, s32[3,384]{1,0:T(4,128)S(1)} %copy-done), custom_call_target="tpu_custom_call" | custom-call | flops 2949120 | bytes 16896 | tf_op jit(solution)/shard_map/order/pallas_call | solution.py:86
  18.0 0.3 collective-permute-done.3.far_ref
  18.3 0.0 copy-done.1
  18.3 0.0 copy-start.2
  18.3 1.0 %copy-done.2 = bf16[16,128,128]{2,1,0:T(8,128)(2,1)S(1)} copy-done((bf16[16,128,128]{2,1,0:T(8,128)(2,1)S(1)}, bf16[16,128,128]{2,1,0:T(8,128)(2,1)}, u32[]{:S(2)}) %copy-start.2) | copy-done | bytes 524312
  19.3 5.9 %table.1 = (f32[8,128,128]{2,1,0:T(8,128)S(1)}, f32[8,128,128]{2,1,0:T(8,128)S(1)}) custom-call(s32[8,384]{1,0:T(8,128)S(1)} %order.1.order_ref, bf16[8,128,128]{2,1,0:T(8,128)(2,1)S(1)} %constant_dynamic-update-slice_fusion.near_ref, bf16[8,128,128]{2,1,0:T(8,128)(2,1)S(1)} %collective-permute-done.3.far_ref, bf16[16,128,128]{2,1,0:T(8,128)(2,1)S(1)} %copy-done.1, ...), custom_call_target="tpu_custom_call" | custom-call | flops 2147483648 | bytes 1048576 | tf_op jit(solution)/shard_map/table/pallas_call | solution.py:167
  25.2 2.0 %collective-permute-start.4 = (f32[8,128,128]{2,1,0:T(8,128)S(1)}, f32[8,128,128]{2,1,0:T(8,128)S(1)}, u32[]{:S(2)}, u32[]{:S(2)}) collective-permute-start(f32[8,128,128]{2,1,0:T(8,128)S(1)} %get-tuple-element.8), channel_id=1, source_target_pairs={{0,1},{1,0},{2,3},{3,2},{4,5},{5,4},{6,7},{7,6},{8,9},{9,8},{10,11... | collective-permute-start | bytes 1572872 | tf_op jit(solution)/shard_map/ppermute | solution.py:203
  27.2 1.5 %collective-permute-done.4 = f32[8,128,128]{2,1,0:T(8,128)S(1)} collective-permute-done((f32[8,128,128]{2,1,0:T(8,128)S(1)}, f32[8,128,128]{2,1,0:T(8,128)S(1)}, u32[]{:S(2)}, u32[]{:S(2)}) %collective-permute-start.4) | collective-permute-done | bytes 524320 | tf_op jit(solution)/shard_map/ppermute | solution.py:203
  28.7 0.1 slice_add_fusion.1
  28.8 0.8 %collective-permute-start.5 = (bf16[4,128,128]{2,1,0:T(8,128)(2,1)S(1)}, bf16[4,128,128]{2,1,0:T(8,128)(2,1)S(1)}, u32[]{:S(2)}, u32[]{:S(2)}) collective-permute-start(bf16[4,128,128]{2,1,0:T(8,128)(2,1)S(1)} %get-tuple-element.10), channel_id=1, source_target_pairs={{0,2},{1,3},{2,0},{3,1},{4,6},{5,7},{6,4},{7,5},{8,10},{9,11},{10,... | collective-permute-start | bytes 393224 | tf_op jit(solution)/shard_map/ppermute | solution.py:203
  29.5 5.1 %collective-permute-done.5 = bf16[4,128,128]{2,1,0:T(8,128)(2,1)S(1)} collective-permute-done((bf16[4,128,128]{2,1,0:T(8,128)(2,1)S(1)}, bf16[4,128,128]{2,1,0:T(8,128)(2,1)S(1)}, u32[]{:S(2)}, u32[]{:S(2)}) %collective-permute-start.5) | collective-permute-done | bytes 131104 | tf_op jit(solution)/shard_map/ppermute | solution.py:203
  34.7 1.8 %collective-permute-start.6 = (bf16[2,128,128]{2,1,0:T(8,128)(2,1)S(1)}, bf16[2,128,128]{2,1,0:T(8,128)(2,1)S(1)}, u32[]{:S(2)}, u32[]{:S(2)}) collective-permute-start(bf16[2,128,128]{2,1,0:T(8,128)(2,1)S(1)} %get-tuple-element.12), channel_id=1, source_target_pairs={{0,4},{1,5},{2,6},{3,7},{4,0},{5,1},{6,2},{7,3},{8,12},{9,13},{10,... | collective-permute-start | bytes 196616 | tf_op jit(solution)/shard_map/ppermute | solution.py:203
  36.5 2.5 %collective-permute-done.6 = bf16[2,128,128]{2,1,0:T(8,128)(2,1)S(1)} collective-permute-done((bf16[2,128,128]{2,1,0:T(8,128)(2,1)S(1)}, bf16[2,128,128]{2,1,0:T(8,128)(2,1)S(1)}, u32[]{:S(2)}, u32[]{:S(2)}) %collective-permute-start.6) | collective-permute-done | bytes 65568 | tf_op jit(solution)/shard_map/ppermute | solution.py:203
  39.0 3.2 %collective-permute-start.7 = (bf16[1,128,128]{2,1,0:T(8,128)(2,1)S(1)}, bf16[1,128,128]{2,1,0:T(8,128)(2,1)S(1)}, u32[]{:S(2)}, u32[]{:S(2)}) collective-permute-start(bf16[1,128,128]{2,1,0:T(8,128)(2,1)S(1)} %fusion.2), channel_id=1, source_target_pairs={{0,8},{1,9},{2,10},{3,11},{4,12},{5,13},{6,14},{7,15},{8,0},{9,1},... | collective-permute-start | bytes 98312 | tf_op jit(solution)/shard_map/ppermute | solution.py:203
  42.2 1.9 %collective-permute-done.7 = bf16[1,128,128]{2,1,0:T(8,128)(2,1)S(1)} collective-permute-done((bf16[1,128,128]{2,1,0:T(8,128)(2,1)S(1)}, bf16[1,128,128]{2,1,0:T(8,128)(2,1)S(1)}, u32[]{:S(2)}, u32[]{:S(2)}) %collective-permute-start.7) | collective-permute-done | bytes 32800 | tf_op jit(solution)/shard_map/ppermute | solution.py:203
  44.1 0.6 %fusion.3 = f32[1,128,128]{2,1,0:T(8,128)} fusion(f32[2,128,128]{2,1,0:T(8,128)S(1)} %convert_element_type.21, f32[2,128,128]{2,1,0:T(8,128)S(1)} %get-tuple-element.11, bf16[1,128,128]{2,1,0:T(8,128)(2,1)S(1)} %collective-permute-done.7), kind=kLoop, calls=%fused_computation.10 | loop fusion | flops 49152 | bytes 229376 | tf_op jit(solution)/shard_map/add | solution.py:221
  (9 shorter events, 0.1 us)
Async XLA Ops:
  0.0 8.8 %copy-start.3 = (bf16[1,128,128]{2,1,0:T(8,128)(2,1)S(1)}, bf16[1,128,128]{2,1,0:T(8,128)(2,1)}, u32[]{:S(2)}) copy-start(bf16[1,128,128]{2,1,0:T(8,128)(2,1)} %param.5) | copy-start | bytes 98308
  0.0 18.3 %copy-start.1 = (bf16[16,128,128]{2,1,0:T(8,128)(2,1)S(1)}, bf16[16,128,128]{2,1,0:T(8,128)(2,1)}, u32[]{:S(2)}) copy-start(bf16[16,128,128]{2,1,0:T(8,128)(2,1)} %left_ref.1) | copy-start | bytes 1572868
  0.0 6.6 %collective-permute-start = (bf16[1,128,128]{2,1,0:T(8,128)(2,1)}, bf16[1,128,128]{2,1,0:T(8,128)(2,1)S(1)}, u32[]{:S(2)}, u32[]{:S(2)}) collective-permute-start(bf16[1,128,128]{2,1,0:T(8,128)(2,1)} %param.5), channel_id=1, source_target_pairs={{0,8},{1,9},{2,10},{3,11},{4,12},{5,13},{6,14},{7,15},{8,0},{9,1},... | collective-permute-start | bytes 98312 | tf_op jit(solution)/shard_map/ppermute | solution.py:203
  7.3 4.3 %collective-permute-start.1 = (bf16[2,128,128]{2,1,0:T(8,128)(2,1)S(1)}, bf16[2,128,128]{2,1,0:T(8,128)(2,1)S(1)}, u32[]{:S(2)}, u32[]{:S(2)}) collective-permute-start(bf16[2,128,128]{2,1,0:T(8,128)(2,1)S(1)} %pad_maximum_fusion.1), channel_id=1, source_target_pairs={{0,4},{1,5},{2,6},{3,7},{4,0},{5,1},{6,2},{7,3},{8,12},{9,13},{10,... | collective-permute-start | bytes 196616 | tf_op jit(solution)/shard_map/ppermute | solution.py:203
  11.6 5.0 %collective-permute-start.2 = (bf16[4,128,128]{2,1,0:T(8,128)(2,1)S(1)}, bf16[4,128,128]{2,1,0:T(8,128)(2,1)S(1)}, u32[]{:S(2)}, u32[]{:S(2)}) collective-permute-start(bf16[4,128,128]{2,1,0:T(8,128)(2,1)S(1)} %pad_maximum_fusion), channel_id=1, source_target_pairs={{0,2},{1,3},{2,0},{3,1},{4,6},{5,7},{6,4},{7,5},{8,10},{9,11},{10,... | collective-permute-start | bytes 393224 | tf_op jit(solution)/shard_map/ppermute | solution.py:203
  16.7 0.7 %copy-start = (s32[3,384]{1,0:T(4,128)S(1)}, s32[3,384]{1,0:T(4,128)}, u32[]{:S(2)}) copy-start(s32[3,384]{1,0:T(4,128)} %refs_2_.1) | copy-start | bytes 13828
  16.7 1.6 %collective-permute-start.3 = (bf16[8,128,128]{2,1,0:T(8,128)(2,1)S(1)}, bf16[8,128,128]{2,1,0:T(8,128)(2,1)S(1)}, u32[]{:S(2)}, u32[]{:S(2)}) collective-permute-start(bf16[8,128,128]{2,1,0:T(8,128)(2,1)S(1)} %constant_dynamic-update-slice_fusion.near_ref), channel_id=1, source_target_pairs={{0,1},{1,0},{2,3},{3,2},{4,5},{5,4},{6,7},{7,6},{8,9},{9,8},{10,11... | collective-permute-start | bytes 786440 | tf_op jit(solution)/shard_map/ppermute | solution.py:203
  18.3 1.0 %copy-start.2 = (bf16[16,128,128]{2,1,0:T(8,128)(2,1)S(1)}, bf16[16,128,128]{2,1,0:T(8,128)(2,1)}, u32[]{:S(2)}) copy-start(bf16[16,128,128]{2,1,0:T(8,128)(2,1)} %right_ref.1) | copy-start | bytes 1572868
  25.2 3.5 %collective-permute-start.4 = (f32[8,128,128]{2,1,0:T(8,128)S(1)}, f32[8,128,128]{2,1,0:T(8,128)S(1)}, u32[]{:S(2)}, u32[]{:S(2)}) collective-permute-start(f32[8,128,128]{2,1,0:T(8,128)S(1)} %get-tuple-element.8), channel_id=1, source_target_pairs={{0,1},{1,0},{2,3},{3,2},{4,5},{5,4},{6,7},{7,6},{8,9},{9,8},{10,11... | collective-permute-start | bytes 1572872 | tf_op jit(solution)/shard_map/ppermute | solution.py:203
  28.8 5.8 %collective-permute-start.5 = (bf16[4,128,128]{2,1,0:T(8,128)(2,1)S(1)}, bf16[4,128,128]{2,1,0:T(8,128)(2,1)S(1)}, u32[]{:S(2)}, u32[]{:S(2)}) collective-permute-start(bf16[4,128,128]{2,1,0:T(8,128)(2,1)S(1)} %get-tuple-element.10), channel_id=1, source_target_pairs={{0,2},{1,3},{2,0},{3,1},{4,6},{5,7},{6,4},{7,5},{8,10},{9,11},{10,... | collective-permute-start | bytes 393224 | tf_op jit(solution)/shard_map/ppermute | solution.py:203
  34.7 4.3 %collective-permute-start.6 = (bf16[2,128,128]{2,1,0:T(8,128)(2,1)S(1)}, bf16[2,128,128]{2,1,0:T(8,128)(2,1)S(1)}, u32[]{:S(2)}, u32[]{:S(2)}) collective-permute-start(bf16[2,128,128]{2,1,0:T(8,128)(2,1)S(1)} %get-tuple-element.12), channel_id=1, source_target_pairs={{0,4},{1,5},{2,6},{3,7},{4,0},{5,1},{6,2},{7,3},{8,12},{9,13},{10,... | collective-permute-start | bytes 196616 | tf_op jit(solution)/shard_map/ppermute | solution.py:203
  39.0 5.0 %collective-permute-start.7 = (bf16[1,128,128]{2,1,0:T(8,128)(2,1)S(1)}, bf16[1,128,128]{2,1,0:T(8,128)(2,1)S(1)}, u32[]{:S(2)}, u32[]{:S(2)}) collective-permute-start(bf16[1,128,128]{2,1,0:T(8,128)(2,1)S(1)} %fusion.2), channel_id=1, source_target_pairs={{0,8},{1,9},{2,10},{3,11},{4,12},{5,13},{6,14},{7,15},{8,0},{9,1},... | collective-permute-start | bytes 98312 | tf_op jit(solution)/shard_map/ppermute | solution.py:203

commit v4 on v3

v4 whole, which is shorter than its diff:
```python
import jax
import jax.numpy as jnp
from jax import lax
from jax.experimental import pallas as pl
from jax.experimental.pallas import tpu as pltpu
from jax.sharding import PartitionSpec as P

VMEM = pl.BlockSpec(memory_space=pltpu.VMEM)
SMEM = pl.BlockSpec(memory_space=pltpu.SMEM)

BLOCKS, CELL_BLOCK, SUM_FIRST, SUM_COUNT, ENDS = range(5)


def transposed_dot(a, b):
    return lax.dot_general(
        a, b, (((1,), (1,)), ((), ())), preferred_element_type=jnp.float32
    )


def iota(shape, axis):
    return lax.broadcasted_iota(jnp.int32, shape, axis)


def count(mask, axis):
    return jnp.sum(mask.astype(jnp.float32), axis=axis, keepdims=True).astype(jnp.int32)


def picked(mask, values, axis):
    kept = jnp.where(mask, values, 0).astype(jnp.float32)
    return jnp.sum(kept, axis=axis, keepdims=True).astype(jnp.int32)


def as_column(row):
    n = row.shape[1]
    return picked(iota((n, n), 0) == iota((n, n), 1), row, 1)


def order_kernel(chips, nops, me_ref, live_ref, coup_ref, right_ref, out_ref, turned_ref):
    slots = coup_ref.shape[1]
    m = right_ref.shape[1]
    cells = 2 * chips * nops
    me = me_ref[0]

    def place(sector):
        return ((sector ^ me) & 1) * chips + (sector >> 1)

    g = coup_ref[0:1, :]
    alive = iota((1, slots), 1) < live_ref[0]
    cell = jnp.where(alive, place(coup_ref[2:3, :]) * nops + g, cells)
    block = place(coup_ref[1:2, :]) * nops + g
    cell_col = as_column(cell)
    block_col = as_column(block)
    square = (slots, slots)
    ahead = (cell < cell_col) | ((cell == cell_col) & (iota(square, 1) < iota(square, 0)))
    spot_col = count(ahead, 1)
    out_ref[BLOCKS : BLOCKS + 1, :] = picked(spot_col == iota(square, 1), block_col, 0)

    lane = iota((1, cells), 1)
    first = count(cell_col < lane, 0)
    here = cell_col == lane
    number = count(here, 0)
    only = picked(here, block_col, 0)
    few = (number <= 4).astype(jnp.int32) + (number <= 2).astype(jnp.int32)
    kind = jnp.where(number < 2, 6, few + jnp.where(lane < cells // 2, 3, 0))
    square = (cells, cells)
    kind_col = as_column(kind)
    ahead = (kind_col < kind) | ((kind_col == kind) & (iota(square, 0) < iota(square, 1)))
    spot = count(ahead, 0)
    cell_block = jnp.where(number == 0, cells, jnp.where(number == 1, only, cells + 1 + spot))
    chosen = as_column(spot) == iota(square, 1)
    out_ref[CELL_BLOCK : CELL_BLOCK + 1, :cells] = cell_block
    out_ref[SUM_FIRST : SUM_FIRST + 1, :cells] = picked(chosen, as_column(first), 0)
    out_ref[SUM_COUNT : SUM_COUNT + 1, :cells] = picked(chosen, as_column(number), 0)
    small = iota((1, 128), 1)
    ends = jnp.zeros((1, 128), jnp.int32)
    for k in range(6):
        ends = jnp.where(small == k, count(kind <= k, 1), ends)
    out_ref[ENDS : ENDS + 1, :128] = ends

    for g in range(nops):
        turned_ref[g * m : (g + 1) * m] = right_ref[g].T


def order_slots(chips, right_ops, couplings, live, me):
    slots = couplings.shape[1]
    nops, m, _ = right_ops.shape
    cells = 2 * chips * nops
    return pl.pallas_call(
        lambda *refs: order_kernel(chips, nops, *refs),
        out_shape=[
            jax.ShapeDtypeStruct((8, max(slots, cells)), jnp.int32),
            jax.ShapeDtypeStruct((nops * m, m), jnp.bfloat16),
        ],
        in_specs=[SMEM, SMEM, VMEM, VMEM],
        out_specs=[VMEM, VMEM],
        compiler_params=pltpu.CompilerParams(vmem_limit_bytes=16 * 1024 * 1024),
        cost_estimate=pl.CostEstimate(
            flops=20 * slots * slots, bytes_accessed=4 * nops * m * m, transcendentals=0
        ),
        name="order",
    )(me, live, couplings, right_ops)


def add_up(order_ref, block_ref, cells, begin, ends):
    many, some, two = ends
    m = block_ref.shape[1]

    @pl.loop(begin, many)
    def _(k):
        first = order_ref[SUM_FIRST, k]

        def add(j, total):
            return total + block_ref[order_ref[BLOCKS, first + j]].astype(jnp.float32)

        total = lax.fori_loop(0, order_ref[SUM_COUNT, k], add, jnp.zeros((m, m), jnp.float32))
        block_ref[cells + 1 + k] = total.astype(jnp.bfloat16)

    @pl.loop(many, some)
    def _(k):
        first = order_ref[SUM_FIRST, k]
        fourth = jnp.where(order_ref[SUM_COUNT, k] == 4, order_ref[BLOCKS, first + 3], cells)
        total = block_ref[order_ref[BLOCKS, first]].astype(jnp.float32)
        total += block_ref[order_ref[BLOCKS, first + 1]].astype(jnp.float32)
        total += block_ref[order_ref[BLOCKS, first + 2]].astype(jnp.float32)
        total += block_ref[fourth].astype(jnp.float32)
        block_ref[cells + 1 + k] = total.astype(jnp.bfloat16)

    @pl.loop(some, two, step=2)
    def _(k):
        ks = (k, jnp.minimum(k + 1, two - 1))
        firsts = [order_ref[SUM_FIRST, k] for k in ks]
        totals = [
            block_ref[order_ref[BLOCKS, first]] + block_ref[order_ref[BLOCKS, first + 1]]
            for first in firsts
        ]
        for k, total in zip(ks, totals):
            block_ref[cells + 1 + k] = total


def multiply(order_ref, block_ref, turned_ref, out_ref, offset, nops):
    half, m, _ = out_ref.shape
    for t in range(0, half, 2):
        rows = [
            jnp.concatenate(
                [
                    block_ref[order_ref[CELL_BLOCK, (offset + t + i) * nops + g]]
                    for g in range(nops)
                ],
                axis=1,
            )
            for i in range(2)
        ]
        out = jnp.dot(
            jnp.concatenate(rows, axis=0), turned_ref[...], preferred_element_type=jnp.float32
        )
        out_ref[t : t + 2] = out.reshape(2, m, m)


def first_kernel(order_ref, near_ref, far_ref, left_ref, turned_ref, block_ref, send_ref):
    nops, m, _ = left_ref.shape
    half = near_ref.shape[0]
    cells = 2 * half * nops

    step = 4
    for s in range(0, 2 * half, 2):
        psi_ref = near_ref if s < half else far_ref
        pair = jnp.concatenate([psi_ref[s % half], psi_ref[s % half + 1]], axis=1)
        for g in range(0, nops, step):
            rows = left_ref[g : g + step].reshape(step * m, m)
            both = jnp.dot(rows, pair, preferred_element_type=jnp.float32).astype(jnp.bfloat16)
            at = s * nops + g
            block_ref[at : at + step] = both[:, :m].reshape(step, m, m)
            block_ref[at + nops : at + nops + step] = both[:, m:].reshape(step, m, m)
    block_ref[cells] = jnp.zeros((m, m), jnp.bfloat16)

    add_up(order_ref, block_ref, cells, 0, [order_ref[ENDS, k] for k in range(3)])
    multiply(order_ref, block_ref, turned_ref, send_ref, half, nops)


def second_kernel(nops, order_ref, _, turned_ref, block_ref, keep_ref):
    half = keep_ref.shape[0]
    ends = [order_ref[ENDS, k] for k in range(2, 6)]
    add_up(order_ref, block_ref, 2 * half * nops, ends[0], ends[1:])
    multiply(order_ref, block_ref, turned_ref, keep_ref, 0, nops)


def first_part(near, far, left_ops, turned, order):
    half = near.shape[0]
    nops, m, _ = left_ops.shape
    cells = 2 * half * nops
    slots = order.shape[1]
    return pl.pallas_call(
        first_kernel,
        out_shape=[
            jax.ShapeDtypeStruct((cells + 1 + slots // 2, m, m), jnp.bfloat16),
            jax.ShapeDtypeStruct((half, m, m), jnp.float32),
        ],
        in_specs=[SMEM] + [VMEM] * 4,
        out_specs=[VMEM, VMEM],
        compiler_params=pltpu.CompilerParams(vmem_limit_bytes=24 * 1024 * 1024),
        cost_estimate=pl.CostEstimate(
            flops=4 * cells * m**3, bytes_accessed=4 * nops * m * m, transcendentals=0
        ),
        name="first",
    )(order, near, far, left_ops, turned)


def second_part(half, blocks, turned, order):
    m = blocks.shape[1]
    nops = turned.shape[0] // m
    return pl.pallas_call(
        lambda *refs: second_kernel(nops, *refs),
        out_shape=[
            jax.ShapeDtypeStruct(blocks.shape, blocks.dtype),
            jax.ShapeDtypeStruct((half, m, m), jnp.float32),
        ],
        in_specs=[SMEM, VMEM, VMEM],
        out_specs=[VMEM, VMEM],
        input_output_aliases={1: 0},
        compiler_params=pltpu.CompilerParams(vmem_limit_bytes=24 * 1024 * 1024),
        cost_estimate=pl.CostEstimate(
            flops=4 * half * nops * m**3, bytes_accessed=4 * nops * m * m, transcendentals=0
        ),
        name="second",
    )(order, blocks, turned)[1]


def slot_kernel(live_ref, coup_ref, psi_ref, left_ref, right_ref, out_ref):
    out_ref[...] = jnp.zeros_like(out_ref)

    @pl.loop(0, live_ref[0])
    def _(c):
        g = coup_ref[0, c]
        half = jnp.dot(left_ref[g], psi_ref[coup_ref[1, c]], preferred_element_type=jnp.float32)
        out_ref[coup_ref[2, c]] += transposed_dot(half.astype(jnp.bfloat16), right_ref[g])


def by_slot(whole, left_ops, right_ops, couplings, live):
    return pl.pallas_call(
        slot_kernel,
        out_shape=jax.ShapeDtypeStruct(whole.shape, jnp.float32),
        in_specs=[SMEM] * 2 + [VMEM] * 3,
        out_specs=VMEM,
        compiler_params=pltpu.CompilerParams(vmem_limit_bytes=60 * 1024 * 1024),
        name="slots",
    )(live, couplings, whole, left_ops, right_ops)


def swap(x, ops, d):
    return lax.ppermute(x, "ops", [(i, i ^ d) for i in range(ops)])


def shards_small(ops, psi, left_ops, right_ops, couplings, live):
    chips = ops // 2
    me = lax.axis_index("ops").astype(jnp.int32)
    same_core = [list(range(core, ops, 2)) for core in range(2)]
    order, turned = order_slots(chips, right_ops, couplings, live, me[None])
    copies = jnp.broadcast_to(psi, (chips, *psi.shape[1:]))
    near = lax.all_to_all(copies, "ops", 0, 0, axis_index_groups=same_core, tiled=True)
    far = swap(near, ops, 1)
    blocks, send = first_part(near, far, left_ops, turned, order)
    came = swap(send, ops, 1)
    keep = second_part(chips, blocks, turned, order)
    chip = keep + came
    parts = lax.all_to_all(
        chip.astype(jnp.bfloat16), "ops", 0, 0, axis_index_groups=same_core, tiled=True
    )
    own = (jnp.arange(chips, dtype=jnp.int32) == me >> 1)[:, None, None]
    return jnp.sum(jnp.where(own, chip, parts.astype(jnp.float32)), axis=0, keepdims=True)


def shards_large(psi, left_ops, right_ops, couplings, live):
    whole = lax.all_gather(psi, "ops", axis=0, tiled=True)
    total = by_slot(whole, left_ops, right_ops, couplings, live)
    return lax.psum_scatter(total, "ops", scatter_dimension=0, tiled=True)


def solution(mesh):
    ops = mesh.shape["ops"]
    placed = (
        P(("groups", "ops"), None, None),
        P(("groups", "ops"), None, None),
        P(("groups", "ops"), None, None),
        P(None, ("groups", "ops")),
        P(("groups", "ops")),
    )

    def shards(psi, *rest):
        small = psi.shape[0] == 1 and 4 <= ops <= 16 and ops & (ops - 1) == 0
        if small:
            return shards_small(ops, psi, *rest)
        return shards_large(psi, *rest)

    return jax.shard_map(
        shards,
        mesh=mesh,
        in_specs=placed,
        out_specs=P(("groups", "ops"), None, None),
        check_vma=False,
    )
```

time: 45.3 us -> 44.7 us (0.987)
  blocking collectives: 0 us -> 16 us
  starting transfers between devices: 15 us -> 3.86 us
  waiting for transfers between devices: 19.8 us -> 9.27 us
  Pallas kernels: 6.46 us -> 8.96 us
  local copies, waits for them, and re-layouts: 1.1 us -> 3.56 us
    ppermute x8 -> x2, waiting for transfers between devices: 19.8 us -> 0.01 us  [swap(): return lax.ppermute(x, 'ops', [(i, i ^ d) for i in range(ops)])]
    all_to_all x0 -> x1, blocking collectives: none -> 16 us  [shards_small(): lax.all_to_all(copies, 'ops', 0, 0, axis_index_groups=same_core, tiled=True)]
    ppermute x8 -> x2, starting transfers between devices: 15 us -> 0.1 us  [swap(): return lax.ppermute(x, 'ops', [(i, i ^ d) for i in range(ops)])]
    all_to_all x0 -> x1, waiting for transfers between devices: none -> 9.26 us  [shards_small(): lax.all_to_all(chip.astype(jnp.bfloat16), 'ops', 0, 0, axis_index_groups=...]
    all_to_all x0 -> x1, starting transfers between devices: none -> 3.77 us  [shards_small(): lax.all_to_all(chip.astype(jnp.bfloat16), 'ops', 0, 0, axis_index_groups=...]
    pallas_call x2 -> x3, Pallas kernels: 6.46 us -> 8.96 us  [the longest x1 5.32 us: first_part(): pl.pallas_call(first_kernel, out_shape=[jax.ShapeDtypeStruct((cells + 1 +...]
    unnamed x11 -> x6, local copies, waits for them, and re-layouts: 1.08 us -> 2.76 us
    broadcast_in_dim x0 -> x1, local copies, waits for them, and re-layouts: none -> 0.79 us  [shards_small(): copies = jnp.broadcast_to(psi, (chips, *psi.shape[1:]))]
  transfers between devices with their start and end apart: 8 -> 3, of which waited for: 8 -> 1; matrix products, arithmetic and copies ran while one was open for 0% -> 0% of each run, Pallas kernels for 1% -> 8%
where the time goes in v4:
time: 44.7 us; the launch traced here: 43.9 us
  blocking collectives  16 us (36%)
  waiting for transfers between devices  9.27 us (21%)
  Pallas kernels  8.96 us (20%)
  starting transfers between devices  3.86 us (9%)
  local copies, waits for them, and re-layouts  3.56 us (8%)
  other arithmetic  1.54 us (3%)
  between operations  0.71 us (2%)
    all_to_all x1, blocking collectives, shards_small(): lax.all_to_all(copies, 'ops', 0, 0, axis_index_groups=same_core, tiled=True)  16 us
    all_to_all x1, waiting for transfers between devices, shards_small(): lax.all_to_all(chip.astype(jnp.bfloat16), 'ops', 0, 0, axis_index_groups=...  9.26 us
    pallas_call x1, Pallas kernels, first_part(): pl.pallas_call(first_kernel, out_shape=[jax.ShapeDtypeStruct((cells + 1 +...  5.32 us
    all_to_all x1, starting transfers between devices, shards_small(): lax.all_to_all(chip.astype(jnp.bfloat16), 'ops', 0, 0, axis_index_groups=...  3.77 us
    pallas_call x1, Pallas kernels, second_part(): pl.pallas_call(lambda *refs: second_kernel(nops, *refs), out_shape=[jax.S...  2.88 us
    unnamed x6, local copies, waits for them, and re-layouts  2.76 us
  transfers between devices with their start and end apart: 3, of which 1 were waited for; matrix products, arithmetic and copies ran while one was open for 0% of the time, Pallas kernels for 8%

profile of v4, /device:TPU:0, one launch (start us, length us, event | category | flops | bytes accessed | tf_op | source)
XLA Modules:
  0.0 43.9 jit_solution(6198596778306066943)
XLA Ops:
  0.0 0.8 %broadcast_in_dim.25 = bf16[8,128,128]{2,1,0:T(8,128)(2,1)S(1)} broadcast(bf16[128,128]{1,0:T(8,128)(2,1)} %bitcast.3), dimensions={1,2} | broadcast | bytes 294912 | tf_op jit(solution)/shard_map/broadcast_in_dim | solution.py:258
  0.8 16.0 %all_to_all.10.near_ref = bf16[8,128,128]{2,1,0:T(8,128)(2,1)S(1)} all-to-all(bf16[8,128,128]{2,1,0:T(8,128)(2,1)S(1)} %broadcast_in_dim.25), channel_id=1, replica_groups={{0,2,4,6,8,10,12,14},{1,3,5,7,9,11,13,15},{16,18,20,22,24,26,28,30},{17..., dimensions={0} | all-to-all | bytes 524288 | tf_op jit(solution)/shard_map/all_to_all | solution.py:259
  16.8 0.0 collective-permute-start
  17.4 0.0 copy-start
  17.4 1.0 %copy-done = bf16[16,128,128]{2,1,0:T(8,128)(2,1)S(1)} copy-done((bf16[16,128,128]{2,1,0:T(8,128)(2,1)S(1)}, bf16[16,128,128]{2,1,0:T(8,128)(2,1)}, u32[]{:S(2)}) %copy-start) | copy-done | bytes 524312
  18.5 0.0 copy-start.1
  18.5 0.7 %copy-done.1 = s32[3,384]{1,0:T(4,128)S(1)} copy-done((s32[3,384]{1,0:T(4,128)S(1)}, s32[3,384]{1,0:T(4,128)}, u32[]{:S(2)}) %copy-start.1) | copy-done | bytes 4632
  19.2 0.8 %order.1 = (s32[8,384]{1,0:T(8,128)S(1)}, bf16[2048,128]{1,0:T(8,128)(2,1)S(1)}) custom-call(s32[1]{0:T(128)} %bitcast.refs_0_, s32[1]{0:T(128)S(6)} %copy.8.refs_1_, s32[3,384]{1,0:T(4,128)S(1)} %copy-done.1, bf16[16,128,128]{2,1,0:T(8,128)(2,1)S(1)} %copy-done), custom_call_target="tpu_custom_call" | custom-call | flops 2949120 | bytes 1048576 | tf_op jit(solution)/shard_map/order/pallas_call | solution.py:88
  19.9 0.0 collective-permute-done.far_ref
  19.9 0.0 copy-start.2
  19.9 1.0 %copy-done.2 = bf16[16,128,128]{2,1,0:T(8,128)(2,1)S(1)} copy-done((bf16[16,128,128]{2,1,0:T(8,128)(2,1)S(1)}, bf16[16,128,128]{2,1,0:T(8,128)(2,1)}, u32[]{:S(2)}) %copy-start.2) | copy-done | bytes 524312
  21.0 5.3 %first.1 = (bf16[449,128,128]{2,1,0:T(8,128)(2,1)S(1)}, f32[8,128,128]{2,1,0:T(8,128)S(1)}) custom-call(s32[8,384]{1,0:T(8,128)S(1)} %get-tuple-element.10.order_ref.refs_0_, bf16[8,128,128]{2,1,0:T(8,128)(2,1)S(1)} %all_to_all.10.near_ref, bf16[8,128,128]{2,1,0:T(8,128)(2,1)S(1)} %collective-permute-done.far_ref, bf16[16,128,128]{2,1,0:T(8,128)(2,1)S(1)} %copy-done.2, ...), custom_call_target="tpu_custom_call" | custom-call | flops 2147483648 | bytes 1048576 | tf_op jit(solution)/shard_map/first/pallas_call | solution.py:192
  26.3 0.1 collective-permute-start.1
  26.4 2.9 %second.1 = (bf16[449,128,128]{2,1,0:T(8,128)(2,1)S(1)}, f32[8,128,128]{2,1,0:T(8,128)S(1)}) custom-call(s32[8,384]{1,0:T(8,128)S(1)} %get-tuple-element.10.order_ref.refs_0_, bf16[449,128,128]{2,1,0:T(8,128)(2,1)S(1)} %get-tuple-element.12.refs_1_, bf16[2048,128]{1,0:T(8,128)(2,1)S(1)} %get-tuple-element.11.turned_ref.refs_2_), custom_call_target="tpu_custom_call", output_to_operand_aliasing={{0}: (1, {})} | custom-call | flops 1073741824 | bytes 1048576 | tf_op jit(solution)/shard_map/second/pallas_call | solution.py:211
  29.3 0.0 collective-permute-done.1
  29.3 0.8 %fusion = (bf16[8,128,128]{2,1,0:T(8,128)(2,1)}, f32[8,128,128]{2,1,0:T(8,128)S(1)}) fusion(f32[8,128,128]{2,1,0:T(8,128)S(1)} %get-tuple-element.13, f32[8,128,128]{2,1,0:T(8,128)S(1)} %collective-permute-done.1), kind=kLoop, calls=%fused_computation.2 | loop fusion | flops 262144 | bytes 1835008 | tf_op jit(solution)/shard_map/convert_element_type | solution.py:266
  30.1 3.8 %all-to-all-start.1 = ((bf16[8,128,128]{2,1,0:T(8,128)(2,1)}), bf16[8,128,128]{2,1,0:T(8,128)(2,1)S(1)}, u32[]{:S(2)}, u32[]{:S(2)}) async-start(bf16[8,128,128]{2,1,0:T(8,128)(2,1)} %get-tuple-element.15), calls=%async_computation.1 | async-start | bytes 524288 | tf_op jit(solution)/shard_map/all_to_all | solution.py:265
  33.9 9.3 %all-to-all-done.1 = bf16[8,128,128]{2,1,0:T(8,128)(2,1)S(1)} async-done(((bf16[8,128,128]{2,1,0:T(8,128)(2,1)}), bf16[8,128,128]{2,1,0:T(8,128)(2,1)S(1)}, u32[]{:S(2)}, u32[]{:S(2)}) %all-to-all-start.1) | async-done | bytes 262176 | tf_op jit(solution)/shard_map/all_to_all | solution.py:265
  43.1 0.7 %select_reduce_fusion = f32[128,128]{1,0:T(8,128)} fusion(f32[8,128,128]{2,1,0:T(8,128)S(1)} %get-tuple-element.16, bf16[8,128,128]{2,1,0:T(8,128)(2,1)S(1)} %all-to-all-done.1, pred[8]{0:T(512)(128)(4,1)S(1)} %iota_compare_fusion), kind=kLoop, calls=%fused_computation | loop fusion | flops 376832 | bytes 851976 | tf_op jit(solution)/shard_map/reduce_sum | solution.py:269
  (1 shorter events, 0.0 us)
Async XLA Ops:
  16.8 3.2 %collective-permute-start = (bf16[8,128,128]{2,1,0:T(8,128)(2,1)S(1)}, bf16[8,128,128]{2,1,0:T(8,128)(2,1)S(1)}, u32[]{:S(2)}, u32[]{:S(2)}) collective-permute-start(bf16[8,128,128]{2,1,0:T(8,128)(2,1)S(1)} %all_to_all.10.near_ref), channel_id=1, source_target_pairs={{0,1},{1,0},{2,3},{3,2},{4,5},{5,4},{6,7},{7,6},{8,9},{9,8},{10,11... | collective-permute-start | bytes 786440 | tf_op jit(solution)/shard_map/ppermute | solution.py:250
  17.4 1.0 %copy-start = (bf16[16,128,128]{2,1,0:T(8,128)(2,1)S(1)}, bf16[16,128,128]{2,1,0:T(8,128)(2,1)}, u32[]{:S(2)}) copy-start(bf16[16,128,128]{2,1,0:T(8,128)(2,1)} %refs_3_.1) | copy-start | bytes 1572868
  18.5 0.7 %copy-start.1 = (s32[3,384]{1,0:T(4,128)S(1)}, s32[3,384]{1,0:T(4,128)}, u32[]{:S(2)}) copy-start(s32[3,384]{1,0:T(4,128)} %refs_2_.1) | copy-start | bytes 13828
  19.9 1.0 %copy-start.2 = (bf16[16,128,128]{2,1,0:T(8,128)(2,1)S(1)}, bf16[16,128,128]{2,1,0:T(8,128)(2,1)}, u32[]{:S(2)}) copy-start(bf16[16,128,128]{2,1,0:T(8,128)(2,1)} %left_ref.1) | copy-start | bytes 1572868
  26.3 3.0 %collective-permute-start.1 = (f32[8,128,128]{2,1,0:T(8,128)S(1)}, f32[8,128,128]{2,1,0:T(8,128)S(1)}, u32[]{:S(2)}, u32[]{:S(2)}) collective-permute-start(f32[8,128,128]{2,1,0:T(8,128)S(1)} %get-tuple-element.14), channel_id=1, source_target_pairs={{0,1},{1,0},{2,3},{3,2},{4,5},{5,4},{6,7},{7,6},{8,9},{9,8},{10,11... | collective-permute-start | bytes 1572872 | tf_op jit(solution)/shard_map/ppermute | solution.py:250
  30.1 13.0 %all-to-all-start.1 = ((bf16[8,128,128]{2,1,0:T(8,128)(2,1)}), bf16[8,128,128]{2,1,0:T(8,128)(2,1)S(1)}, u32[]{:S(2)}, u32[]{:S(2)}) async-start(bf16[8,128,128]{2,1,0:T(8,128)(2,1)} %get-tuple-element.15), calls=%async_computation.1 | async-start | bytes 524288 | tf_op jit(solution)/shard_map/all_to_all | solution.py:265
